TPU v7x, 32 devices: a whole 2x2x4 slice. The times are simulated.
32 devices in a mesh: wide: 4 (over z), narrow: 8 (over y, x, core).
Axes of the slice: x: 2, y: 2, z: 4, core: 2. Of those that a mesh axis runs over, the one named last changes fastest.
Arguments:
- frames: bfloat16 [16384, 2048], P('narrow', 'wide'), may hold values from -6 to 6
- weights: bfloat16 [2, 2048, 2048], P(None, 'narrow', 'wide'), may hold values from -0.125 to 0.125
- gains: float32 [2, 2048], P(None, 'wide'), may hold values from 0.1 to 1.9
- shifts: float32 [2, 2048], P(None, 'wide'), may hold values from -3 to 3
- decays: float32 [2, 2048], P(None, 'wide'), may hold values from 0.3 to 0.97
- resets: int32 [16384], P('narrow'), may hold values 0 or 1
- running: float32 [2, 2, 2048], P(None, None, 'wide'), may hold values from 0.5 to 2
- grad_out: bfloat16 [16384, 2048], P('narrow', 'wide'), may hold values from -6 to 6
Outputs:
- activations: bfloat16 [16384, 2048], P('narrow', 'wide')
- input_grad: float32 [16384, 2048], P('narrow', 'wide')
- weight_grad: float32 [2, 2048, 2048], P(None, 'narrow', 'wide')
- gain_grad: float32 [2, 2048], P(None, 'wide')
- shift_grad: float32 [2, 2048], P(None, 'wide')
- decay_grad: float32 [2, 2048], P(None, 'wide')
- running_new: float32 [2, 2, 2048], P(None, None, 'wide')
All inputs are finite; a program needn't handle non-finite values. No bound on the sum of `resets` on one device may be relied on, other than what follows from the above.
Results may differ from a plain program's by a relative error of at most 0.0047.
Values may be sent and summed in bfloat16 or wider, within the bound.
No kernel may reach another device: no remote copies, remote signals or barrier semaphores. Data moves between devices by JAX's collectives and lax.ppermute only.
A program may use at most 192 MiB of HBM per device.

v0:
```python
import jax
import jax.numpy as jnp
from jax import lax
from jax.sharding import PartitionSpec as P

LENGTH = 1024


eps_norm = 1e-05
momentum = 0.1


def link(earlier, later):
    return (earlier[0] * later[0], later[0] * earlier[1] + later[1])


def per_device(frames, weights, gains, shifts, decays, resets, running, grad_out):
    frame_rows, lanes = frames.shape
    count = frame_rows * lax.axis_size("narrow") * 1.0
    keep = (1 - resets).astype(jnp.float32).reshape(-1, LENGTH, 1)
    layer_in = frames
    saved = []
    updated = []
    for level in range(2):
        full_in = lax.all_gather(layer_in, "wide", axis=1, tiled=True)
        full_weight = lax.all_gather(weights[level], "narrow", axis=0, tiled=True)
        pre = jnp.dot(full_in, full_weight, preferred_element_type=jnp.float32)
        total, squares = lax.psum((jnp.sum(pre, 0), jnp.sum(pre * pre, 0)), "narrow")
        mean = total / count
        var = squares / count - mean * mean
        scale = lax.rsqrt(var + eps_norm)
        normed_hat = (pre - mean) * scale
        drive = (normed_hat * gains[level] + shifts[level]).reshape(-1, LENGTH, lanes)
        rate = keep * decays[level]
        _, states = lax.associative_scan(link, (rate, drive), axis=1)
        saved.append((full_in, full_weight, normed_hat, scale, states, rate))
        states = states.reshape(frame_rows, lanes)
        layer_in = jax.nn.silu(states).astype(jnp.bfloat16)
        new_mean = (1.0 - momentum) * running[level, 0] + momentum * mean
        new_var = (1.0 - momentum) * running[level, 1] + momentum * var * count / (count - 1.0)
        updated.append(jnp.stack([new_mean, new_var]))
    grad = grad_out.astype(jnp.float32)
    weight_list = [None, None]
    gain_list = [None, None]
    shift_list = [None, None]
    decay_list = [None, None]
    for level in (1, 0):
        full_in, full_weight, normed_hat, scale, states, rate = saved[level]
        sigma = jax.nn.sigmoid(states)
        grad_state = grad.reshape(-1, LENGTH, lanes) * (sigma + states * sigma * (1.0 - sigma))
        rate_next = jnp.concatenate([rate[:, 1:], jnp.zeros_like(rate[:, :1])], axis=1)
        _, carried = lax.associative_scan(link, (rate_next, grad_state), reverse=True, axis=1)
        prior = jnp.concatenate([jnp.zeros_like(states[:, :1]), states[:, :-1]], axis=1)
        decay_term = jnp.sum(carried * keep * prior, axis=(0, 1))
        carried = carried.reshape(frame_rows, lanes)
        shift_sum, gain_sum, decay_sum = lax.psum(
            (jnp.sum(carried, 0), jnp.sum(carried * normed_hat, 0), decay_term), "narrow"
        )
        grad_pre = (
            gains[level] * scale * (carried - shift_sum / count - normed_hat * gain_sum / count)
        ).astype(jnp.bfloat16)
        weight_list[level] = lax.psum_scatter(
            lax.dot_general(
                full_in, grad_pre, (((0,), (0,)), ((), ())), preferred_element_type=jnp.float32
            ),
            "narrow",
            scatter_dimension=0,
            tiled=True,
        )
        gain_list[level] = gain_sum
        shift_list[level] = shift_sum
        decay_list[level] = decay_sum
        partial_term = lax.dot_general(
            grad_pre, full_weight, (((1,), (1,)), ((), ())), preferred_element_type=jnp.float32
        )
        grad = lax.psum_scatter(partial_term, "wide", scatter_dimension=1, tiled=True)
    return (
        layer_in,
        grad,
        jnp.stack(weight_list),
        jnp.stack(gain_list),
        jnp.stack(shift_list),
        jnp.stack(decay_list),
        jnp.stack(updated),
    )


def solution(mesh):
    placed = (
        P("narrow", "wide"),
        P(None, "narrow", "wide"),
        P(None, "wide"),
        P(None, "wide"),
        P(None, "wide"),
        P("narrow"),
        P(None, None, "wide"),
        P("narrow", "wide"),
    )
    return jax.shard_map(
        per_device,
        mesh=mesh,
        in_specs=placed,
        out_specs=(
            P("narrow", "wide"),
            P("narrow", "wide"),
            P(None, "narrow", "wide"),
            P(None, "wide"),
            P(None, "wide"),
            P(None, "wide"),
            P(None, None, "wide"),
        ),
        check_vma=False,
    )
```

profile of v0, /device:TPU:28, one launch (start us, length us, event | category | flops | bytes accessed | tf_op | source)
XLA Modules:
  0.0 1842.9 jit_solution(15407598178813647526)
XLA Ops:
  27.6 11.7 slice.1018
  39.3 11.9 slice.1017
  52.4 135.4 %all-gather.7.cloned.1.call-done = bf16[2048,2048]{1,0:T(8,128)(2,1)} async-done(((bf16[2048,512]{1,0:T(8,128)(2,1)}), bf16[2048,2048]{1,0:T(8,128)(2,1)}) %all-gather.7.cloned.1.call-update) | async-done | bytes 8388624 | tf_op jit(solution)/shard_map/all_gather | solution.py:25
  198.3 13.2 all-reduce.87
  217.1 11.8 slice.1090
  355.8 11.7 slice.1101
  379.2 11.8 slice.1096
  429.6 16.6 slice.1182
  446.2 17.2 slice.1173
  473.9 28.9 %all-gather.9.cloned.1.call-done = bf16[2048,2048]{1,0:T(8,128)(2,1)} async-done(((bf16[2048,512]{1,0:T(8,128)(2,1)}), bf16[2048,2048]{1,0:T(8,128)(2,1)}) %all-gather.9.cloned.1.call-update) | async-done | bytes 8388624 | tf_op jit(solution)/shard_map/all_gather | solution.py:25
  513.6 13.3 all-reduce.86
  532.4 11.8 slice.1169
  707.3 16.7 slice.1177
  877.2 32.7 %rev.4 = f32[2,1024,512]{2,1,0:T(8,128)} reverse(f32[2,1024,512]{2,1,0:T(8,128)} %add.699), dimensions={1} | reverse | bytes 8388608 | tf_op jit(solution)/shard_map/rev | solution.py:52
  917.3 11.8 all-reduce.85
  982.5 16.7 slice.1264
  999.2 17.2 slice.1255
  1043.2 180.8 %reduce-scatter.5.cloned.1.call-done = f32[2048,512]{1,0:T(8,128)} async-done(((f32[2048,2048]{1,0:T(8,128)}), f32[2048,512]{1,0:T(8,128)}) %reduce-scatter.5.cloned.1.call-update) | async-done | bytes 4194320 | tf_op jit(solution)/shard_map/reduce_scatter | solution.py:76
  1231.6 11.9 slice.1332
  1265.5 16.8 slice.1259
  1434.6 32.6 %rev.5 = f32[2,1024,512]{2,1,0:T(8,128)} reverse(f32[2,1024,512]{2,1,0:T(8,128)} %add.730), dimensions={1} | reverse | bytes 8388608 | tf_op jit(solution)/shard_map/rev | solution.py:52
  1473.8 13.0 all-reduce.84
  1519.2 33.5 %reduce-scatter.9.cloned.1.call-done = f32[256,512]{0,1:T(8,128)} async-done(((f32[2048,512]{0,1:T(8,128)}), f32[256,512]{0,1:T(8,128)}) %reduce-scatter.9.cloned.1.call-update) | async-done | bytes 524304 | tf_op jit(solution)/shard_map/reduce_scatter | solution.py:62
  1555.2 280.6 %reduce-scatter.7.cloned.1.call-done = f32[2048,512]{1,0:T(8,128)} async-done(((f32[2048,2048]{1,0:T(8,128)}), f32[2048,512]{1,0:T(8,128)}) %reduce-scatter.7.cloned.1.call-update) | async-done | bytes 4194320 | tf_op jit(solution)/shard_map/reduce_scatter | solution.py:76
  (683 shorter events, 866.8 us)
Async XLA Ops:
  7.2 45.2 %all-gather.11.cloned.1.call-start = ((), (), s32[]{:S(2)}) async-start(), calls=%async_computation.10 | async-start | bytes 2359296 | tf_op jit(solution)/shard_map/all_gather | solution.py:26
  9.1 178.6 %all-gather.7.cloned.1.call-start = ((), (), s32[]{:S(2)}) async-start(), calls=%async_computation.4 | async-start | bytes 10485760 | tf_op jit(solution)/shard_map/all_gather | solution.py:25
  9.8 464.1 %all-gather.13.cloned.1.call-start = ((), (), s32[]{:S(2)}) async-start(), calls=%async_computation.11 | async-start | bytes 2359296 | tf_op jit(solution)/shard_map/all_gather | solution.py:26
  10.6 492.2 %all-gather.9.cloned.1.call-start = ((), (), s32[]{:S(2)}) async-start(), calls=%async_computation.5 | async-start | bytes 10485760 | tf_op jit(solution)/shard_map/all_gather | solution.py:25
  27.6 23.6 %copy-start.77 = (f32[2,512]{1,0:T(2,128)S(1)}, f32[2,512]{1,0:T(2,128)}, u32[]{:S(2)}) copy-start(f32[2,512]{1,0:T(2,128)} %param.10) | copy-start | bytes 12292
  27.6 23.6 %copy-start.78 = (f32[2,512]{1,0:T(2,128)S(1)}, f32[2,512]{1,0:T(2,128)}, u32[]{:S(2)}) copy-start(f32[2,512]{1,0:T(2,128)} %param.11) | copy-start | bytes 12292
  27.6 24.2 %copy-start.68 = (f32[2,2,512]{2,1,0:T(2,128)S(1)}, f32[2,2,512]{2,1,0:T(2,128)}, u32[]{:S(2)}) copy-start(f32[2,2,512]{2,1,0:T(2,128)} %param.14) | copy-start | bytes 24580
  355.7 868.3 %reduce-scatter.5.cloned.1.call-start = ((), (), s32[]{:S(2)}) async-start(), calls=%async_computation.6 | async-start | bytes 20971520 | tf_op jit(solution)/shard_map/reduce_scatter | solution.py:76
  473.9 53.0 %copy-start.73 = (f32[1,1,512]{2,1,0:T(1,128)S(1)}, f32[1,1,512]{2,1,0:T(1,128)}, u32[]{:S(2)}) copy-start(f32[1,1,512]{2,1,0:T(1,128)} %get-tuple-element.110) | copy-start | bytes 6148
  473.9 53.0 %copy-start.74 = (f32[1,1,512]{2,1,0:T(1,128)S(1)}, f32[1,1,512]{2,1,0:T(1,128)}, u32[]{:S(2)}) copy-start(f32[1,1,512]{2,1,0:T(1,128)} %get-tuple-element.111) | copy-start | bytes 6148
  473.9 53.6 %copy-start.64 = (f32[1,512]{1,0:T(1,128)S(1)}, f32[1,512]{1,0:T(1,128)}, u32[]{:S(2)}) copy-start(f32[1,512]{1,0:T(1,128)} %get-tuple-element.132) | copy-start | bytes 6148
  786.8 27.2 %copy-start.23 = (f32[2,511,512]{2,1,0:T(8,128)S(1)}, f32[2,511,512]{2,1,0:T(8,128)}, u32[]{:S(2)}) copy-start(f32[2,511,512]{2,1,0:T(8,128)} %slice.1250) | copy-start | bytes 6279172
  814.0 19.8 %copy-start.40 = (f32[2,63,512]{2,1,0:T(8,128)S(1)}, f32[2,63,512]{2,1,0:T(8,128)}, u32[]{:S(2)}) copy-start(f32[2,63,512]{2,1,0:T(8,128)} %slice.1195) | copy-start | bytes 774148
  877.2 32.7 %copy-start.51 = (f32[512]{0:T(512)S(1)}, f32[512]{0:T(512)}, u32[]{:S(2)}) copy-start(f32[512]{0:T(512)} %copy-done.50) | copy-start | bytes 6148
  877.2 32.7 %copy-start.53 = (f32[512]{0:T(512)S(1)}, f32[512]{0:T(512)}, u32[]{:S(2)}) copy-start(f32[512]{0:T(512)} %copy-done.52) | copy-start | bytes 6148
  877.2 37.0 %copy-start.45 = (f32[2,1024]{1,0:T(2,128)S(1)}, f32[2,1024]{1,0:T(2,128)}, u32[]{:S(2)}) copy-start(f32[2,1024]{1,0:T(2,128)} %copy-done.44) | copy-start | bytes 24580
  915.8 13.3 copy-start.63
  943.7 575.5 %reduce-scatter.11.cloned.1.call-start = ((), (), s32[]{:S(2)}) async-start(), calls=%async_computation.9 | async-start | bytes 4718592 | tf_op jit(solution)/shard_map/reduce_scatter | solution.py:62
  1043.1 509.5 %reduce-scatter.9.cloned.1.call-start = ((), (), s32[]{:S(2)}) async-start(), calls=%async_computation.8 | async-start | bytes 4718592 | tf_op jit(solution)/shard_map/reduce_scatter | solution.py:62
  1345.0 27.2 %copy-start.24 = (f32[2,511,512]{2,1,0:T(8,128)S(1)}, f32[2,511,512]{2,1,0:T(8,128)}, u32[]{:S(2)}) copy-start(f32[2,511,512]{2,1,0:T(8,128)} %slice.1332) | copy-start | bytes 6279172
  1372.2 19.2 %copy-start.41 = (f32[2,63,512]{2,1,0:T(8,128)S(1)}, f32[2,63,512]{2,1,0:T(8,128)}, u32[]{:S(2)}) copy-start(f32[2,63,512]{2,1,0:T(8,128)} %slice.1277) | copy-start | bytes 774148
  1411.7 10.2 copy-start.14
  1473.1 13.7 copy-start.62
  1501.1 334.8 %reduce-scatter.7.cloned.1.call-start = ((), (), s32[]{:S(2)}) async-start(), calls=%async_computation.7 | async-start | bytes 20971520 | tf_op jit(solution)/shard_map/reduce_scatter | solution.py:76
  (64 other events, 267.2 us)
Sparse Core Ops, SparseCore 0:
  10.5 28.7 all-gather.10
  40.8 146.8 all-gather.6
  189.6 28.8 all-gather.12
  355.8 146.9 all-gather.8
  943.8 280.1 reduce-scatter.4
  1227.6 52.2 reduce-scatter.10
  1501.2 51.4 reduce-scatter.8
  1555.7 280.0 reduce-scatter.6
where the time goes:
time: 1870 us; the launch traced here: 1840 us
  local copies, waits for them, and re-layouts  851 us (46%)
  waiting for transfers between devices  661 us (35%)
  other arithmetic  204 us (11%)
  matrix products  59.5 us (3%)
  blocking collectives  51.4 us (3%)
    reduce_scatter x2, waiting for transfers between devices, per_device(): lax.psum_scatter(partial_term, 'wide', scatter_dimension=1, tiled=True)  461 us
    slice x132, local copies, waits for them, and re-layouts, per_device(): lax.associative_scan(link, (rate_next, grad_state), reverse=True, axis=1)  427 us
    slice x120, local copies, waits for them, and re-layouts, per_device(): _, states = lax.associative_scan(link, (rate, drive), axis=1)  224 us
    all_gather x2, waiting for transfers between devices, per_device(): full_in = lax.all_gather(layer_in, 'wide', axis=1, tiled=True)  164 us
    rev x2, local copies, waits for them, and re-layouts, per_device(): lax.associative_scan(link, (rate_next, grad_state), reverse=True, axis=1)  65.3 us
    mul x32, other arithmetic, link(): return (earlier[0] * later[0], later[0] * earlier[1] + later[1])  52.7 us
    pad x36, local copies, waits for them, and re-layouts, per_device(): lax.associative_scan(link, (rate_next, grad_state), reverse=True, axis=1)  51 us
    pad x36, local copies, waits for them, and re-layouts, per_device(): _, states = lax.associative_scan(link, (rate, drive), axis=1)  50.4 us
  transfers between devices with their start and end apart: 8, of which 5 were waited for; matrix products, arithmetic and copies ran while one was open for 37% of the time, Pallas kernels for 0%

commit v1 on v0

--- a/solution.py
+++ b/solution.py
@@ -1,6 +1,10 @@
+import functools
+
 import jax
 import jax.numpy as jnp
 from jax import lax
+from jax.experimental import pallas as pl
+from jax.experimental.pallas import tpu as pltpu
 from jax.sharding import PartitionSpec as P
 
 LENGTH = 1024
@@ -9,12 +13,394 @@
 eps_norm = 1e-05
 momentum = 0.1
 
+f32 = jnp.float32
+bf16 = jnp.bfloat16
+BIG = 56 * 2**20
+AXES = ("wide", "narrow")
+
+
+def whole(space=pltpu.VMEM):
+    return pl.BlockSpec(memory_space=space)
+
+
+def stats_of(sums, count):
+    mean = sums[0] / count
+    var = sums[1] / count - mean * mean
+    return mean, var, lax.rsqrt(var + eps_norm)
+
+
+def product_kernel(xs, xo, ws, wo, pre, sums):
+    acc = jnp.dot(xs[...], ws[...], preferred_element_type=f32)
+    acc = acc + jnp.dot(xo[...], wo[...], preferred_element_type=f32)
+    parts = acc.shape[1] // 128
+    for g in range(acc.shape[0] // 8):
+        for k in range(parts):
+            pre[pl.ds(g * 8 * parts + k, 8, stride=parts), :] = acc[g * 8 : g * 8 + 8, k * 128 : k * 128 + 128]
+
+    @pl.when(pl.program_id(0) == 0)
+    def _():
+        sums[...] = jnp.zeros_like(sums)
+
+    sums[0:1, :] += jnp.sum(acc, 0, keepdims=True)
+    sums[1:2, :] += jnp.sum(acc * acc, 0, keepdims=True)
+
+
+def product(xs, xo, ws, wo, step=256):
+    rows, depth = xs.shape
+    cols = ws.shape[1]
+    parts = cols // 128
+    pre, sums = pl.pallas_call(
+        product_kernel,
+        grid=(rows // step,),
+        in_specs=[
+            pl.BlockSpec((step, depth), lambda i: (i, 0)),
+            pl.BlockSpec((step, depth), lambda i: (i, 0)),
+            pl.BlockSpec((depth, cols), lambda i: (0, 0)),
+            pl.BlockSpec((depth, cols), lambda i: (0, 0)),
+        ],
+        out_specs=[
+            pl.BlockSpec((step * parts, 128), lambda i: (i, 0)),
+            pl.BlockSpec((2, cols), lambda i: (0, 0)),
+        ],
+        out_shape=[
+            jax.ShapeDtypeStruct((rows * parts, 128), f32),
+            jax.ShapeDtypeStruct((2, cols), f32),
+        ],
+        compiler_params=pltpu.CompilerParams(vmem_limit_bytes=BIG),
+        cost_estimate=pl.CostEstimate(flops=4 * rows * depth * cols, bytes_accessed=12 << 20, transcendentals=0),
+    )(xs, xo, ws, wo)
+    return pre, sums.reshape(2, parts, 128)
+
+
+def forward_kernel(count, sums, params, keep, pre, states, y):
+    mean, _, rstd = stats_of(sums, count)
+    sc = params[0] * rstd
+    sh = params[1] - mean * sc
+    decay = params[2]
+    parts = sc.shape[0]
+    rows = y.shape[0]
+
+    def step(i, h):
+        for u in range(8):
+            t = i * 8 + u
+            at = pl.ds(pl.multiple_of(t * parts, parts), parts)
+            h = (decay * keep[t]) * h + (pre[at, :] * sc + sh)
+            states[at, :] = h
+        return h
+
+    lax.fori_loop(0, rows // 8, step, jnp.zeros_like(sc))
+
+    def turn(g, _):
+        for k in range(parts):
+            two = []
+            for u in range(2):
+                h = states[pl.ds((g * 2 + u) * 8 * parts + k, 8, stride=parts), :]
+                two.append(h / (1.0 + jnp.exp(-h)))
+            y[pl.ds(pl.multiple_of(g * 16, 16), 16), k * 128 : k * 128 + 128] = jnp.concatenate(two, 0).astype(bf16)
+        return 0
+
+    lax.fori_loop(0, rows // 16, turn, 0)
+
+
+def forward(sums, params, keep, pre, count):
+    parts = params.shape[1]
+    rows = pre.shape[0] // parts
+    return pl.pallas_call(
+        functools.partial(forward_kernel, count),
+        in_specs=[whole(), whole(), whole(pltpu.SMEM), whole()],
+        out_specs=[whole(), whole()],
+        out_shape=[
+            jax.ShapeDtypeStruct(pre.shape, f32),
+            jax.ShapeDtypeStruct((rows, parts * 128), bf16),
+        ],
+        compiler_params=pltpu.CompilerParams(vmem_limit_bytes=BIG),
+        cost_estimate=pl.CostEstimate(flops=12 * pre.size, bytes_accessed=10 * pre.size, transcendentals=pre.size),
+    )(sums, params, keep, pre)
+
+
+def backward_kernel(count, n_dy, sums, params, keep, pre, states, *rest):
+    dys, (carried, totals, dyt) = rest[:n_dy], rest[n_dy:]
+    mean, _, rstd = stats_of(sums, count)
+    shift = -mean * rstd
+    decay = params[2]
+    parts = decay.shape[0]
+    rows = dys[0].shape[0]
+
+    def turn(g, _):
+        at = pl.ds(pl.multiple_of(g * 16, 16), 16)
+        for k in range(parts):
+            v = dys[0][at, k * 128 : k * 128 + 128].astype(f32)
+            for d in dys[1:]:
+                v = v + d[at, k * 128 : k * 128 + 128].astype(f32)
+            for u in range(2):
+                dyt[pl.ds((g * 2 + u) * 8 * parts + k, 8, stride=parts), :] = v[u * 8 : u * 8 + 8]
+        return 0
+
+    lax.fori_loop(0, rows // 16, turn, 0)
+
+    def one(t, h, prior, carry):
+        back, sg, sx, sd = carry
+        at = pl.ds(pl.multiple_of(t * parts, parts), parts)
+        s = 1.0 / (1.0 + jnp.exp(-h))
+        g = dyt[at, :] * (s + h * s * (1.0 - s)) + back
+        carried[at, :] = g
+        gk = g * keep[t]
+        return (gk * decay, sg + g, sx + g * (pre[at, :] * rstd + shift), sd + gk * prior)
+
+    def get(t):
+        return states[pl.ds(pl.multiple_of(t * parts, parts), parts), :]
+
+    def step(i, carry):
+        for u in range(8):
+            t = rows - 1 - (i * 8 + u)
+            carry = one(t, get(t), get(t - 1), carry)
+        return carry
+
+    zero = jnp.zeros_like(decay)
+    carry = lax.fori_loop(0, rows // 8 - 1, step, (zero, zero, zero, zero))
+    for t in range(7, -1, -1):
+        carry = one(t, get(t), get(t - 1) if t else zero, carry)
+    totals[0], totals[1], totals[2] = carry[1], carry[2], carry[3]
+
+
+def backward(sums, params, keep, pre, states, dys, count):
+    parts = params.shape[1]
+    return pl.pallas_call(
+        functools.partial(backward_kernel, count, len(dys)),
+        in_specs=[whole(), whole(), whole(pltpu.SMEM), whole(), whole()] + [whole()] * len(dys),
+        out_specs=[whole(), whole()],
+        out_shape=[
+            jax.ShapeDtypeStruct(pre.shape, f32),
+            jax.ShapeDtypeStruct((3, parts, 128), f32),
+        ],
+        scratch_shapes=[pltpu.VMEM(pre.shape, f32)],
+        compiler_params=pltpu.CompilerParams(vmem_limit_bytes=BIG),
+        cost_estimate=pl.CostEstimate(flops=24 * pre.size, bytes_accessed=16 * pre.size, transcendentals=pre.size),
+    )(sums, params, keep, pre, states, *dys)
+
+
+def spread_kernel(count, sums, params, totals, carried, pre, ws, wo, dpre, same, other):
+    mean, _, rstd = stats_of(sums, count)
+    sc = params[0] * rstd
+    slope = sc * rstd * (totals[1] / count)
+    c3 = mean * slope - sc * (totals[0] / count)
+    parts = sc.shape[0]
+    for g in range(dpre.shape[0] // 16):
+        for k in range(parts):
+            two = []
+            for u in range(2):
+                at = pl.ds((g * 2 + u) * 8 * parts + k, 8, stride=parts)
+                two.append(sc[k : k + 1] * carried[at, :] - slope[k : k + 1] * pre[at, :] + c3[k : k + 1])
+            dpre[g * 16 : g * 16 + 16, k * 128 : k * 128 + 128] = jnp.concatenate(two, 0).astype(bf16)
+    d = dpre[...]
+    dims = (((1,), (1,)), ((), ()))
+    same[...] = lax.dot_general(d, ws[...], dims, preferred_element_type=f32)
+    other[...] = lax.dot_general(d, wo[...], dims, preferred_element_type=f32).astype(bf16)
+
+
+def spread(sums, params, totals, carried, pre, ws, wo, count, step=256):
+    parts = params.shape[1]
+    rows, cols = pre.shape[0] // parts, parts * 128
+    depth = ws.shape[0]
+    small = pl.BlockSpec((None, parts, 128), lambda i: (0, 0, 0))
+    return pl.pallas_call(
+        functools.partial(spread_kernel, count),
+        grid=(rows // step,),
+        in_specs=[
+            pl.BlockSpec(sums.shape, lambda i: (0, 0, 0)),
+            pl.BlockSpec(params.shape, lambda i: (0, 0, 0)),
+            pl.BlockSpec(totals.shape, lambda i: (0, 0, 0)),
+            pl.BlockSpec((step * parts, 128), lambda i: (i, 0)),
+            pl.BlockSpec((step * parts, 128), lambda i: (i, 0)),
+            pl.BlockSpec((depth, cols), lambda i: (0, 0)),
+            pl.BlockSpec((depth, cols), lambda i: (0, 0)),
+        ],
+        out_specs=[
+            pl.BlockSpec((step, cols), lambda i: (i, 0)),
+            pl.BlockSpec((step, depth), lambda i: (i, 0)),
+            pl.BlockSpec((step, depth), lambda i: (i, 0)),
+        ],
+        out_shape=[
+            jax.ShapeDtypeStruct((rows, cols), bf16),
+            jax.ShapeDtypeStruct((rows, depth), f32),
+            jax.ShapeDtypeStruct((rows, depth), bf16),
+        ],
+        compiler_params=pltpu.CompilerParams(vmem_limit_bytes=BIG),
+        cost_estimate=pl.CostEstimate(flops=4 * rows * depth * cols, bytes_accessed=20 << 20, transcendentals=0),
+    )(sums, params, totals, carried, pre, ws, wo)
+
+
+def paired(frames, weights, gains, shifts, decays, resets, running, grad_out):
+    wide, narrow = lax.axis_size("wide"), lax.axis_size("narrow")
+    rows, lanes = frames.shape
+    half = lanes // 2
+    depth = weights.shape[1]
+    count = rows * narrow * 1.0
+    z = lax.axis_index("wide")
+    n = lax.axis_index("narrow")
+    r, c = n // 2, n % 2
+    slot = 2 * (z % 2) + c
+
+    def send(x, to):
+        pairs = []
+        for a in range(wide):
+            for b in range(narrow):
+                tz, tr, tc = to(a, b // 2, b % 2)
+                pairs.append((a * narrow + b, tz * narrow + tr * 2 + tc))
+        return lax.ppermute(x, AXES, pairs)
+
+    def swap(x):
+        return send(x, lambda a, b, d: (a, b, 1 - d))
+
+    def over_ring(x, m):
+        return send(x, lambda a, b, d: (a, b ^ m, d))
+
+    def over_wide(x, m):
+        return send(x, lambda a, b, d: (a ^ m, b, d))
+
+    def everywhere(x):
+        a1, a2, a3 = over_ring(x, 1), over_ring(x, 2), over_ring(x, 3)
+        x = (x + a1) + (a2 + a3)
+        a1, a2, a3 = over_wide(x, 1), over_wide(x, 2), over_wide(x, 3)
+        return (x + a1) + (a2 + a3)
+
+    def placed(pieces, shape, spots):
+        buf = jnp.zeros(shape, pieces[0].dtype)
+        for piece, spot in zip(pieces, spots, strict=True):
+            buf = lax.dynamic_update_slice(buf, piece, spot)
+        return buf
+
+    def to_rows(x):
+        got = []
+        for m in range(wide):
+            q = z ^ m
+            piece = lax.dynamic_slice(x, ((q // 2) * LENGTH, (q % 2) * half), (LENGTH, half))
+            got.append(send(piece, lambda a, b, d: (2 * d + ((a ^ m) >> 1), b, (a ^ m) & 1)))
+        return got
+
+    def from_rows(x):
+        got = []
+        for m in range(wide):
+            piece = lax.dynamic_slice(x, (0, (slot ^ m) * half), (LENGTH, half))
+            got.append(send(piece, lambda a, b, d: ((2 * (a & 1) + d) ^ m, b, a >> 1)))
+        return got
+
+    def by_slot(pieces, s):
+        return placed(pieces, (LENGTH, wide * half), [(0, (s ^ m) * half) for m in range(wide)])
+
+    def home(pieces):
+        spots = [(((z ^ m) // 2) * LENGTH, ((z ^ m) % 2) * half) for m in range(wide)]
+        return placed(pieces, (rows, lanes), spots)
+
+    def gathered(w):
+        own = lax.dynamic_slice(w, (0, c * half), (depth, half))
+        away = swap(lax.dynamic_slice(w, (0, (1 - c) * half), (depth, half)))
+        both = jnp.stack([own, away])
+        pieces = [both] + [over_wide(both, m) for m in range(1, wide)]
+        line = placed(pieces, (2, depth, wide * half), [(0, 0, (z ^ m) * half) for m in range(wide)])
+        result = []
+        for part, (first, second) in ((line[0], (1, 2)), (line[1], (2, 1))):
+            p1 = over_ring(part, first)
+            p2 = over_ring(part, second)
+            p3 = over_ring(p1, second)
+            spots = [((r ^ m) * depth, 0) for m in (0, first, second, 3)]
+            result.append(placed([part, p1, p2, p3], (4 * depth, wide * half), spots))
+        return result
+
+    def scattered(parts):
+        done = []
+        for part, (first, second) in ((parts[0], (1, 2)), (parts[1], (2, 1))):
+
+            def block(m, part=part):
+                return lax.dynamic_slice(part, ((r ^ m) * depth, 0), (depth, wide * half))
+
+            g3 = over_ring(block(3).astype(bf16), first)
+            g1 = over_ring(block(first).astype(bf16), first)
+            mid = (block(second) + g3.astype(f32)).astype(bf16)
+            g2 = over_ring(mid, second)
+            done.append(block(0) + g1.astype(f32) + g2.astype(f32))
+        line = jnp.stack(done)
+
+        def col(m):
+            return lax.dynamic_slice(line, (0, 0, (z ^ m) * half), (2, depth, half))
+
+        got = [over_wide(col(m).astype(bf16), m).astype(f32) for m in range(1, wide)]
+        total = (col(0) + got[0]) + (got[1] + got[2])
+        own, away = total[0], swap(total[1])
+        return jnp.concatenate([jnp.where(c == 0, own, away), jnp.where(c == 0, away, own)], axis=1)
+
+    theirs = swap(resets)
+    row = jnp.where(c == z // 2, resets, theirs)
+    keep = 1.0 - lax.dynamic_slice(row, ((z % 2) * LENGTH,), (LENGTH,)).astype(f32)
+    vectors = jnp.concatenate([gains, shifts, decays])
+    vectors = lax.dynamic_slice(vectors, (0, c * half), (6, half))
+    pieces = [vectors] + [over_wide(vectors, m) for m in range(1, wide)]
+    vectors = placed(pieces, (6, wide * half), [(0, (z ^ m) * half) for m in range(wide)])
+    vectors = vectors.reshape(3, 2, -1, 128)
+    params = [vectors[:, level] for level in range(2)]
+
+    mats = [gathered(weights[0])]
+    got = to_rows(frames)
+    xs = by_slot(got, slot)
+    xo = by_slot([swap(p) for p in got], slot ^ 1)
+    mats.append(gathered(weights[1]))
+    grads = by_slot(to_rows(grad_out), slot)
+
+    saved = []
+    ins = (xs, xo)
+    for level in range(2):
+        pre, sums = product(*ins, *mats[level])
+        sums = everywhere(sums)
+        states, y = forward(sums, params[level], keep, pre, count)
+        saved.append((ins, pre, sums, states))
+        if level == 0:
+            ins = (y, swap(y))
+    sent = from_rows(y)
+
+    dys = (grads,)
+    weight_list = [None, None]
+    totals_list = [None, None]
+    for level in (1, 0):
+        ins, pre, sums, states = saved[level]
+        carried, totals = backward(sums, params[level], keep, pre, states, dys, count)
+        totals = everywhere(totals)
+        totals_list[level] = totals
+        dpre, same, other = spread(sums, params[level], totals, carried, pre, *mats[level], count)
+        other = swap(other)
+        dys = (same, other)
+        if level == 0:
+            back = from_rows((same + other.astype(f32)).astype(bf16))
+        dims = (((0,), (0,)), ((), ()))
+        weight_list[level] = scattered(
+            [lax.dot_general(x, dpre, dims, preferred_element_type=f32) for x in ins]
+        )
+
+    small = []
+    for level in range(2):
+        mean, var, _ = stats_of(saved[level][2], count)
+        small.append(jnp.concatenate([mean[None], var[None], totals_list[level]]))
+    small = jnp.stack(small).reshape(2, 5, wide, half)
+    small = lax.dynamic_index_in_dim(small, z, 2, keepdims=False)
+    away = swap(small)
+    small = jnp.concatenate([jnp.where(c == 0, small, away), jnp.where(c == 0, away, small)], axis=2)
+    new_mean = (1.0 - momentum) * running[:, 0] + momentum * small[:, 0]
+    new_var = (1.0 - momentum) * running[:, 1] + momentum * small[:, 1] * count / (count - 1.0)
+    return (
+        home(sent),
+        home(back).astype(f32),
+        jnp.stack(weight_list),
+        small[:, 3],
+        small[:, 2],
+        small[:, 4],
+        jnp.stack([new_mean, new_var], axis=1),
+    )
+
 
 def link(earlier, later):
     return (earlier[0] * later[0], later[0] * earlier[1] + later[1])
 
 
-def per_device(frames, weights, gains, shifts, decays, resets, running, grad_out):
+def general(frames, weights, gains, shifts, decays, resets, running, grad_out):
     frame_rows, lanes = frames.shape
     count = frame_rows * lax.axis_size("narrow") * 1.0
     keep = (1 - resets).astype(jnp.float32).reshape(-1, LENGTH, 1)
@@ -85,6 +471,15 @@
     )
 
 
+def per_device(frames, weights, *rest):
+    wide, narrow = lax.axis_size("wide"), lax.axis_size("narrow")
+    rows, lanes = frames.shape
+    one_row_a_chip = 2 * rows == wide * LENGTH and wide == 4 and narrow == 2 * wide
+    if one_row_a_chip and lanes == 2 * weights.shape[1] and wide * lanes == 2048:
+        return paired(frames, weights, *rest)
+    return general(frames, weights, *rest)
+
+
 def solution(mesh):
     placed = (
         P("narrow", "wide"),

time: 1870 us -> 584 us (0.31); the launches traced: 1840 us -> 576 us
  local copies, waits for them, and re-layouts: 851 us -> 83.5 us
  waiting for transfers between devices: 661 us -> 200 us
  other arithmetic: 204 us -> 26.5 us
  starting transfers between devices: 0.32 us -> 162 us
  Pallas kernels: 0 us -> 87.1 us
  blocking collectives: 51.4 us -> 0 us
  matrix products: 59.5 us -> 14 us
    slice x258 -> x2, local copies, waits for them, and re-layouts: 660 us -> 1.07 us  [the longest x1 1.06 us: paired(): mats.append(gathered(weights[1]))]
    reduce_scatter x4 -> x0, waiting for transfers between devices: 495 us -> none  [the longest x2 461 us: per_device(): lax.psum_scatter(partial_term, 'wide', scatter_dimension=1, tiled=True)]
    ppermute x0 -> x92, waiting for transfers between devices: none -> 200 us  [send(): return lax.ppermute(x, AXES, pairs)]
    all_gather x4 -> x0, waiting for transfers between devices: 164 us -> none  [the longest x2 164 us: per_device(): full_in = lax.all_gather(layer_in, 'wide', axis=1, tiled=True)]
    ppermute x0 -> x92, starting transfers between devices: none -> 162 us  [send(): return lax.ppermute(x, AXES, pairs)]
    pad x72 -> x0, local copies, waits for them, and re-layouts: 101 us -> none  [the longest x36 51 us: per_device(): lax.associative_scan(link, (rate_next, grad_state), reverse=True, axis=1)]
    pallas_call x0 -> x8, Pallas kernels: none -> 87.1 us  [the longest x2 27.6 us: backward(): pl.pallas_call(functools.partial(backward_kernel, count, len(dys)), in_sp...]
    add x81 -> x11, other arithmetic: 85.9 us -> 5.35 us  [the longest x4 2.41 us: everywhere(): return x + a1 + (a2 + a3)]
  transfers between devices with their start and end apart: 8 -> 92, of which waited for: 5 -> 36; matrix products, arithmetic and copies ran while one was open for 37% -> 16% of each run, Pallas kernels for 0% -> 8%
where the time goes in v1:
time: 584 us; the launch traced here: 576 us
  waiting for transfers between devices  200 us (34%)
  starting transfers between devices  162 us (28%)
  Pallas kernels  87.1 us (15%)
  local copies, waits for them, and re-layouts  83.5 us (14%)
  other arithmetic  26.5 us (5%)
  matrix products  14 us (2%)
    ppermute x92, waiting for transfers between devices, send(): return lax.ppermute(x, AXES, pairs)  200 us
    ppermute x92, starting transfers between devices, send(): return lax.ppermute(x, AXES, pairs)  162 us
    dynamic_update_slice x44, local copies, waits for them, and re-layouts, placed(): buf = lax.dynamic_update_slice(buf, piece, spot)  56.4 us
    pallas_call x2, Pallas kernels, backward(): pl.pallas_call(functools.partial(backward_kernel, count, len(dys)), in_sp...  27.6 us
    pallas_call x2, Pallas kernels, forward(): pl.pallas_call(functools.partial(forward_kernel, count), in_specs=[whole(...  20.5 us
    pallas_call x2, Pallas kernels, spread(): pl.pallas_call(functools.partial(spread_kernel, count), grid=(rows // ste...  20.2 us
    pallas_call x2, Pallas kernels, product(): pl.pallas_call(product_kernel, grid=(rows // step,), in_specs=[pl.BlockSp...  18.8 us
    dot_general x4, matrix products, paired(): lax.dot_general(x, dpre, dims, preferred_element_type=f32)  14 us
  transfers between devices with their start and end apart: 92, of which 36 were waited for; matrix products, arithmetic and copies ran while one was open for 16% of the time, Pallas kernels for 8%

profile of v1, /device:TPU:28, one launch (start us, length us, event | category | flops | bytes accessed | tf_op | source)
XLA Modules:
  0.0 575.7 jit_solution(17288554897269231542)
XLA Ops:
  19.4 8.5 %collective-permute-done.30 = bf16[2,256,256]{2,1,0:T(8,128)(2,1)S(1)} collective-permute-done((bf16[2,256,256]{2,1,0:T(8,128)(2,1)S(1)}, bf16[2,256,256]{2,1,0:T(8,128)(2,1)S(1)}, u32[]{:S(2)}, u32[]{:S(2)}) %collective-permute-start.30) | collective-permute-done | bytes 262176 | tf_op jit(solution)/shard_map/ppermute | solution.py:250
  33.6 20.2 %collective-permute-start.32 = (bf16[2,256,256]{2,1,0:T(8,128)(2,1)S(1)}, bf16[2,256,256]{2,1,0:T(8,128)(2,1)S(1)}, u32[]{:S(2)}, u32[]{:S(2)}) collective-permute-start(bf16[2,256,256]{2,1,0:T(8,128)(2,1)S(1)} %get-tuple-element.99), channel_id=1, source_target_pairs={{0,24},{1,25},{2,26},{3,27},{4,28},{5,29},{6,30},{7,31},{8,16},{9,... | collective-permute-start | bytes 786440 | tf_op jit(solution)/shard_map/ppermute | solution.py:250
  54.3 23.8 %collective-permute-start.3 = (bf16[1024,256]{1,0:T(8,128)(2,1)S(1)}, bf16[1024,256]{1,0:T(8,128)(2,1)S(1)}, u32[]{:S(2)}, u32[]{:S(2)}) collective-permute-start(bf16[1024,256]{1,0:T(8,128)(2,1)S(1)} %get-tuple-element.85), channel_id=1, source_target_pairs={{0,9},{1,25},{2,11},{3,27},{4,13},{5,29},{6,15},{7,31},{8,8},{9,24... | collective-permute-start | bytes 1572872 | tf_op jit(solution)/shard_map/ppermute | solution.py:250
  83.7 19.9 %collective-permute-done.3 = bf16[1024,256]{1,0:T(8,128)(2,1)S(1)} collective-permute-done((bf16[1024,256]{1,0:T(8,128)(2,1)S(1)}, bf16[1024,256]{1,0:T(8,128)(2,1)S(1)}, u32[]{:S(2)}, u32[]{:S(2)}) %collective-permute-start.3) | collective-permute-done | bytes 524320 | tf_op jit(solution)/shard_map/ppermute | solution.py:250
  109.4 10.3 %collective-permute-done.17 = bf16[256,1024]{1,0:T(8,128)(2,1)S(1)} collective-permute-done((bf16[256,1024]{1,0:T(8,128)(2,1)S(1)}, bf16[256,1024]{1,0:T(8,128)(2,1)S(1)}, u32[]{:S(2)}, u32[]{:S(2)}) %collective-permute-start.17) | collective-permute-done | bytes 524320 | tf_op jit(solution)/shard_map/ppermute | solution.py:250
  122.6 9.4 %shard_map.135 = (f32[8192,128]{1,0:T(8,128)}, f32[2,1024]{1,0:T(2,128)}) custom-call(bf16[1024,1024]{1,0:T(8,128)(2,1)} %copy-done.14, bf16[1024,1024]{1,0:T(8,128)(2,1)} %copy-done.9, bf16[1024,1024]{1,0:T(8,128)(2,1)} %copy-done.8, bf16[1024,1024]{1,0:T(8,128)(2,1)} %copy-done.13), custom_call_target="tpu_custom_call" | custom-call | flops 4294967296 | bytes 12582912 | tf_op jit(solution)/shard_map/pallas_call | solution.py:52
  149.9 10.4 %shard_map.136 = (f32[8192,128]{1,0:T(8,128)}, bf16[1024,1024]{1,0:T(8,128)(2,1)}) custom-call(f32[2,8,128]{2,1,0:T(8,128)} %add_add_fusion.6.sums, f32[3,8,128]{2,1,0:T(8,128)} %get-tuple-element.108.params, f32[1024]{0:T(1024)} %fusion.35.keep, f32[8192,128]{1,0:T(8,128)} %get-tuple-element.26.pre), custom_call_target="tpu_custom_call" | custom-call | flops 12582912 | bytes 10485760 | tf_op jit(solution)/shard_map/pallas_call | solution.py:108
  181.8 10.0 %collective-permute-done.37 = bf16[256,1024]{1,0:T(8,128)(2,1)S(1)} collective-permute-done((bf16[256,1024]{1,0:T(8,128)(2,1)S(1)}, bf16[256,1024]{1,0:T(8,128)(2,1)S(1)}, u32[]{:S(2)}, u32[]{:S(2)}) %collective-permute-start.37) | collective-permute-done | bytes 524320 | tf_op jit(solution)/shard_map/ppermute | solution.py:250
  191.9 9.7 %collective-permute-start.52 = (bf16[1024,256]{1,0:T(8,128)(2,1)S(1)}, bf16[1024,256]{1,0:T(8,128)(2,1)S(1)}, u32[]{:S(2)}, u32[]{:S(2)}) collective-permute-start(bf16[1024,256]{1,0:T(8,128)(2,1)S(1)} %get-tuple-element.77), channel_id=1, source_target_pairs={{0,9},{1,25},{2,11},{3,27},{4,13},{5,29},{6,15},{7,31},{8,8},{9,24... | collective-permute-start | bytes 1572872 | tf_op jit(solution)/shard_map/ppermute | solution.py:250
  203.8 9.4 %shard_map.137 = (f32[8192,128]{1,0:T(8,128)}, f32[2,1024]{1,0:T(2,128)}) custom-call(bf16[1024,1024]{1,0:T(8,128)(2,1)} %get-tuple-element.27.xs, bf16[1024,1024]{1,0:T(8,128)(2,1)} %collective-permute-done.28.xo, bf16[1024,1024]{1,0:T(8,128)(2,1)} %copy-done.11, bf16[1024,1024]{1,0:T(8,128)(2,1)} %copy-done.16), custom_call_target="tpu_custom_call" | custom-call | flops 4294967296 | bytes 12582912 | tf_op jit(solution)/shard_map/pallas_call | solution.py:52
  232.9 10.1 %shard_map.138 = (f32[8192,128]{1,0:T(8,128)}, bf16[1024,1024]{1,0:T(8,128)(2,1)}) custom-call(f32[2,8,128]{2,1,0:T(8,128)} %add_add_fusion.4.sums, f32[3,8,128]{2,1,0:T(8,128)} %get-tuple-element.107.params, f32[1024]{0:T(1024)} %fusion.35.keep, f32[8192,128]{1,0:T(8,128)} %get-tuple-element.29.pre), custom_call_target="tpu_custom_call" | custom-call | flops 12582912 | bytes 10485760 | tf_op jit(solution)/shard_map/pallas_call | solution.py:108
  243.0 13.1 %shard_map.139 = (f32[8192,128]{1,0:T(8,128)}, f32[3,8,128]{2,1,0:T(8,128)}) custom-call(f32[2,8,128]{2,1,0:T(8,128)} %add_add_fusion.4.sums, f32[3,8,128]{2,1,0:T(8,128)} %get-tuple-element.107.params, f32[1024]{0:T(1024)} %fusion.35.keep, f32[8192,128]{1,0:T(8,128)} %get-tuple-element.29.pre, f32[8192,128]{1,0:T(8,128)} %get-tuple-element.32.states, ...), custom_call_target="tpu_custom_call" | custom-call | flops 25165824 | bytes 16777216 | tf_op jit(solution)/shard_map/pallas_call | solution.py:168
  272.6 10.1 %shard_map.140 = (bf16[1024,1024]{1,0:T(8,128)(2,1)}, f32[1024,1024]{1,0:T(8,128)}, bf16[1024,1024]{1,0:T(8,128)(2,1)}) custom-call(f32[2,8,128]{2,1,0:T(8,128)} %add_add_fusion.4.sums, f32[3,8,128]{2,1,0:T(8,128)} %get-tuple-element.107.params, f32[3,8,128]{2,1,0:T(8,128)} %add_add_fusion.2.totals, f32[8192,128]{1,0:T(8,128)} %get-tuple-element.34.carried, ...), custom_call_target="tpu_custom_call" | custom-call | flops 4294967296 | bytes 20971520 | tf_op jit(solution)/shard_map/pallas_call | solution.py:206
  299.5 8.1 %collective-permute-done.82 = bf16[256,1024]{0,1:T(8,128)(2,1)S(1)} collective-permute-done((bf16[256,1024]{0,1:T(8,128)(2,1)S(1)}, bf16[256,1024]{0,1:T(8,128)(2,1)S(1)}, u32[]{:S(2)}, u32[]{:S(2)}) %collective-permute-start.82) | collective-permute-done | bytes 524320 | tf_op jit(solution)/shard_map/ppermute | solution.py:250
  310.9 15.2 %collective-permute-done.86 = bf16[256,1024]{0,1:T(8,128)(2,1)} collective-permute-done((bf16[256,1024]{0,1:T(8,128)(2,1)S(1)}, bf16[256,1024]{0,1:T(8,128)(2,1)}, u32[]{:S(2)}, u32[]{:S(2)}) %collective-permute-start.86) | collective-permute-done | bytes 524320 | tf_op jit(solution)/shard_map/ppermute | solution.py:250
  338.6 14.5 %shard_map.141 = (f32[8192,128]{1,0:T(8,128)}, f32[3,8,128]{2,1,0:T(8,128)}) custom-call(f32[2,8,128]{2,1,0:T(8,128)} %add_add_fusion.6.sums, f32[3,8,128]{2,1,0:T(8,128)} %get-tuple-element.108.params, f32[1024]{0:T(1024)} %fusion.35.keep, f32[8192,128]{1,0:T(8,128)} %get-tuple-element.26.pre, f32[8192,128]{1,0:T(8,128)} %get-tuple-element.31.states, ...), custom_call_target="tpu_custom_call" | custom-call | flops 25165824 | bytes 16777216 | tf_op jit(solution)/shard_map/pallas_call | solution.py:168
  366.0 20.4 %collective-permute-done.64 = f32[3,8,128]{2,1,0:T(8,128)S(1)} collective-permute-done((f32[3,8,128]{2,1,0:T(8,128)S(1)}, f32[3,8,128]{2,1,0:T(8,128)S(1)}, u32[]{:S(2)}, u32[]{:S(2)}) %collective-permute-start.64) | collective-permute-done | bytes 12320 | tf_op jit(solution)/shard_map/ppermute | solution.py:250
  389.1 10.2 %shard_map.142 = (bf16[1024,1024]{1,0:T(8,128)(2,1)}, f32[1024,1024]{1,0:T(8,128)}, bf16[1024,1024]{1,0:T(8,128)(2,1)}) custom-call(f32[2,8,128]{2,1,0:T(8,128)} %add_add_fusion.6.sums, f32[3,8,128]{2,1,0:T(8,128)} %get-tuple-element.108.params, f32[3,8,128]{2,1,0:T(8,128)} %add_add_fusion.totals, f32[8192,128]{1,0:T(8,128)} %get-tuple-element.38.carried, ...), custom_call_target="tpu_custom_call" | custom-call | flops 4294967296 | bytes 20971520 | tf_op jit(solution)/shard_map/pallas_call | solution.py:206
  424.4 7.5 %dynamic_update_slice.182 = bf16[2048,512]{1,0:T(8,128)(2,1)S(1)} dynamic-update-slice(bf16[2048,512]{1,0:T(8,128)(2,1)S(1)} %dynamic_update_slice.181, bf16[1024,256]{1,0:T(8,128)(2,1)} %collective-permute-done.47, s32[]{:T(128)S(6)} %select_n.298, s32[]{:T(128)S(6)} %select_n.300) | dynamic-update-slice | bytes 1048580 | tf_op jit(solution)/shard_map/dynamic_update_slice | solution.py:270
  432.0 8.3 %dynamic_update_slice.183 = bf16[2048,512]{1,0:T(8,128)(2,1)S(1)} dynamic-update-slice(bf16[2048,512]{1,0:T(8,128)(2,1)S(1)} %dynamic_update_slice.182, bf16[1024,256]{1,0:T(8,128)(2,1)} %collective-permute-done.48, s32[]{:T(128)S(6)} %select_n.303, s32[]{:T(128)S(6)} %select_n.305) | dynamic-update-slice | bytes 1048580 | tf_op jit(solution)/shard_map/dynamic_update_slice | solution.py:270
  456.6 11.8 %collective-permute-done.76 = bf16[256,1024]{0,1:T(8,128)(2,1)} collective-permute-done((bf16[256,1024]{0,1:T(8,128)(2,1)}, bf16[256,1024]{0,1:T(8,128)(2,1)}, u32[]{:S(2)}, u32[]{:S(2)}) %collective-permute-start.76) | collective-permute-done | bytes 524320 | tf_op jit(solution)/shard_map/ppermute | solution.py:250
  483.9 11.3 %collective-permute-done.78 = bf16[2,256,256]{1,2,0:T(8,128)(2,1)S(1)} collective-permute-done((bf16[2,256,256]{1,2,0:T(8,128)(2,1)S(1)}, bf16[2,256,256]{1,2,0:T(8,128)(2,1)S(1)}, u32[]{:S(2)}, u32[]{:S(2)}) %collective-permute-start.78) | collective-permute-done | bytes 262176 | tf_op jit(solution)/shard_map/ppermute | solution.py:250
  526.4 26.7 %collective-permute-done.68 = bf16[1024,256]{1,0:T(8,128)(2,1)S(1)} collective-permute-done((bf16[1024,256]{1,0:T(8,128)(2,1)}, bf16[1024,256]{1,0:T(8,128)(2,1)S(1)}, u32[]{:S(2)}, u32[]{:S(2)}) %collective-permute-start.68) | collective-permute-done | bytes 524320 | tf_op jit(solution)/shard_map/ppermute | solution.py:250
  565.0 7.6 %dynamic_update_slice.191 = bf16[2048,512]{1,0:T(8,128)(2,1)S(1)} dynamic-update-slice(bf16[2048,512]{1,0:T(8,128)(2,1)S(1)} %dynamic_update_slice.190, bf16[1024,256]{1,0:T(8,128)(2,1)S(1)} %collective-permute-done.70, s32[]{:T(128)S(6)} %select_n.303, s32[]{:T(128)S(6)} %select_n.305) | dynamic-update-slice | bytes 1048580 | tf_op jit(solution)/shard_map/dynamic_update_slice | solution.py:270
  (361 shorter events, 266.7 us)
Async XLA Ops:
  10.0 69.5 %collective-permute-start = (bf16[1024,256]{1,0:T(8,128)(2,1)}, bf16[1024,256]{1,0:T(8,128)(2,1)S(1)}, u32[]{:S(2)}, u32[]{:S(2)}) collective-permute-start(bf16[1024,256]{1,0:T(8,128)(2,1)} %get-tuple-element.87), channel_id=1, source_target_pairs={{0,0},{1,16},{2,2},{3,18},{4,4},{5,20},{6,6},{7,22},{8,1},{9,17},{... | collective-permute-start | bytes 1572872 | tf_op jit(solution)/shard_map/ppermute | solution.py:250
  14.8 38.9 %collective-permute-start.9 = (bf16[2,256,256]{2,1,0:T(8,128)(2,1)S(1)}, bf16[2,256,256]{2,1,0:T(8,128)(2,1)S(1)}, u32[]{:S(2)}, u32[]{:S(2)}) collective-permute-start(bf16[2,256,256]{2,1,0:T(8,128)(2,1)S(1)} %get-tuple-element.103), channel_id=1, source_target_pairs={{0,8},{1,9},{2,10},{3,11},{4,12},{5,13},{6,14},{7,15},{8,0},{9,1},... | collective-permute-start | bytes 786440 | tf_op jit(solution)/shard_map/ppermute | solution.py:250
  16.8 37.1 %collective-permute-start.10 = (bf16[2,256,256]{2,1,0:T(8,128)(2,1)S(1)}, bf16[2,256,256]{2,1,0:T(8,128)(2,1)S(1)}, u32[]{:S(2)}, u32[]{:S(2)}) collective-permute-start(bf16[2,256,256]{2,1,0:T(8,128)(2,1)S(1)} %get-tuple-element.103), channel_id=1, source_target_pairs={{0,16},{1,17},{2,18},{3,19},{4,20},{5,21},{6,22},{7,23},{8,24},{9,... | collective-permute-start | bytes 786440 | tf_op jit(solution)/shard_map/ppermute | solution.py:250
  33.6 44.6 %collective-permute-start.32 = (bf16[2,256,256]{2,1,0:T(8,128)(2,1)S(1)}, bf16[2,256,256]{2,1,0:T(8,128)(2,1)S(1)}, u32[]{:S(2)}, u32[]{:S(2)}) collective-permute-start(bf16[2,256,256]{2,1,0:T(8,128)(2,1)S(1)} %get-tuple-element.99), channel_id=1, source_target_pairs={{0,24},{1,25},{2,26},{3,27},{4,28},{5,29},{6,30},{7,31},{8,16},{9,... | collective-permute-start | bytes 786440 | tf_op jit(solution)/shard_map/ppermute | solution.py:250
  53.8 27.6 %collective-permute-start.1 = (bf16[1024,256]{1,0:T(8,128)(2,1)S(1)}, bf16[1024,256]{1,0:T(8,128)(2,1)S(1)}, u32[]{:S(2)}, u32[]{:S(2)}) collective-permute-start(bf16[1024,256]{1,0:T(8,128)(2,1)S(1)} %copy-done.19), channel_id=1, source_target_pairs={{0,1},{1,17},{2,3},{3,19},{4,5},{5,21},{6,7},{7,23},{8,0},{9,16},{... | collective-permute-start | bytes 1572872 | tf_op jit(solution)/shard_map/ppermute | solution.py:250
  53.9 28.2 %collective-permute-start.2 = (bf16[1024,256]{1,0:T(8,128)(2,1)S(1)}, bf16[1024,256]{1,0:T(8,128)(2,1)S(1)}, u32[]{:S(2)}, u32[]{:S(2)}) collective-permute-start(bf16[1024,256]{1,0:T(8,128)(2,1)S(1)} %get-tuple-element.88), channel_id=1, source_target_pairs={{0,8},{1,24},{2,10},{3,26},{4,12},{5,28},{6,14},{7,30},{8,9},{9,25... | collective-permute-start | bytes 1572872 | tf_op jit(solution)/shard_map/ppermute | solution.py:250
  54.3 49.3 %collective-permute-start.3 = (bf16[1024,256]{1,0:T(8,128)(2,1)S(1)}, bf16[1024,256]{1,0:T(8,128)(2,1)S(1)}, u32[]{:S(2)}, u32[]{:S(2)}) collective-permute-start(bf16[1024,256]{1,0:T(8,128)(2,1)S(1)} %get-tuple-element.85), channel_id=1, source_target_pairs={{0,9},{1,25},{2,11},{3,27},{4,13},{5,29},{6,15},{7,31},{8,8},{9,24... | collective-permute-start | bytes 1572872 | tf_op jit(solution)/shard_map/ppermute | solution.py:250
  109.1 36.4 %collective-permute-start.27 = (s32[2048]{0:T(1024)S(1)}, s32[2048]{0:T(1024)S(1)}, u32[]{:S(2)}, u32[]{:S(2)}) collective-permute-start(s32[2048]{0:T(1024)S(1)} %copy-done.30), channel_id=1, source_target_pairs={{0,1},{1,0},{2,3},{3,2},{4,5},{5,4},{6,7},{7,6},{8,9},{9,8},{10,11... | collective-permute-start | bytes 24584 | tf_op jit(solution)/shard_map/ppermute | solution.py:250
  160.3 41.5 %collective-permute-start.28 = (bf16[1024,1024]{1,0:T(8,128)(2,1)}, bf16[1024,1024]{1,0:T(8,128)(2,1)}, u32[]{:S(2)}, u32[]{:S(2)}) collective-permute-start(bf16[1024,1024]{1,0:T(8,128)(2,1)} %get-tuple-element.27.xs), channel_id=1, source_target_pairs={{0,1},{1,0},{2,3},{3,2},{4,5},{5,4},{6,7},{7,6},{8,9},{9,8},{10,11... | collective-permute-start | bytes 6291464 | tf_op jit(solution)/shard_map/ppermute | solution.py:250
  191.9 37.3 %collective-permute-start.52 = (bf16[1024,256]{1,0:T(8,128)(2,1)S(1)}, bf16[1024,256]{1,0:T(8,128)(2,1)S(1)}, u32[]{:S(2)}, u32[]{:S(2)}) collective-permute-start(bf16[1024,256]{1,0:T(8,128)(2,1)S(1)} %get-tuple-element.77), channel_id=1, source_target_pairs={{0,9},{1,25},{2,11},{3,27},{4,13},{5,29},{6,15},{7,31},{8,8},{9,24... | collective-permute-start | bytes 1572872 | tf_op jit(solution)/shard_map/ppermute | solution.py:250
  295.8 41.5 %collective-permute-start.59 = (bf16[1024,1024]{1,0:T(8,128)(2,1)}, bf16[1024,1024]{1,0:T(8,128)(2,1)S(1)}, u32[]{:S(2)}, u32[]{:S(2)}) collective-permute-start(bf16[1024,1024]{1,0:T(8,128)(2,1)} %get-tuple-element.36), channel_id=1, source_target_pairs={{0,1},{1,0},{2,3},{3,2},{4,5},{5,4},{6,7},{7,6},{8,9},{9,8},{10,11... | collective-permute-start | bytes 6291464 | tf_op jit(solution)/shard_map/ppermute | solution.py:250
  296.3 31.4 %collective-permute-start.81 = (bf16[256,1024]{0,1:T(8,128)(2,1)}, bf16[256,1024]{0,1:T(8,128)(2,1)}, u32[]{:S(2)}, u32[]{:S(2)}) collective-permute-start(bf16[256,1024]{0,1:T(8,128)(2,1)} %get-tuple-element.65), channel_id=1, source_target_pairs={{0,2},{1,3},{2,0},{3,1},{4,6},{5,7},{6,4},{7,5},{8,10},{9,11},{10,... | collective-permute-start | bytes 1572872 | tf_op jit(solution)/shard_map/ppermute | solution.py:250
  297.9 28.2 %collective-permute-start.86 = (bf16[256,1024]{0,1:T(8,128)(2,1)S(1)}, bf16[256,1024]{0,1:T(8,128)(2,1)}, u32[]{:S(2)}, u32[]{:S(2)}) collective-permute-start(bf16[256,1024]{0,1:T(8,128)(2,1)S(1)} %add_convert_fusion.1), channel_id=1, source_target_pairs={{0,2},{1,3},{2,0},{3,1},{4,6},{5,7},{6,4},{7,5},{8,10},{9,11},{10,... | collective-permute-start | bytes 1572872 | tf_op jit(solution)/shard_map/ppermute | solution.py:250
  335.3 69.2 %collective-permute-start.45 = (bf16[1024,256]{1,0:T(8,128)(2,1)S(1)}, bf16[1024,256]{1,0:T(8,128)(2,1)S(1)}, u32[]{:S(2)}, u32[]{:S(2)}) collective-permute-start(bf16[1024,256]{1,0:T(8,128)(2,1)S(1)} %get-tuple-element.84), channel_id=1, source_target_pairs={{0,0},{1,8},{2,2},{3,10},{4,4},{5,12},{6,6},{7,14},{8,16},{9,24},{... | collective-permute-start | bytes 1572872 | tf_op jit(solution)/shard_map/ppermute | solution.py:250
  337.3 74.1 %collective-permute-start.46 = (bf16[1024,256]{1,0:T(8,128)(2,1)S(1)}, bf16[1024,256]{1,0:T(8,128)(2,1)S(1)}, u32[]{:S(2)}, u32[]{:S(2)}) collective-permute-start(bf16[1024,256]{1,0:T(8,128)(2,1)S(1)} %get-tuple-element.83), channel_id=1, source_target_pairs={{0,8},{1,0},{2,10},{3,2},{4,12},{5,4},{6,14},{7,6},{8,24},{9,16},{... | collective-permute-start | bytes 1572872 | tf_op jit(solution)/shard_map/ppermute | solution.py:250
  364.5 59.9 %collective-permute-start.47 = (bf16[1024,256]{1,0:T(8,128)(2,1)}, bf16[1024,256]{1,0:T(8,128)(2,1)}, u32[]{:S(2)}, u32[]{:S(2)}) collective-permute-start(bf16[1024,256]{1,0:T(8,128)(2,1)} %get-tuple-element.82), channel_id=1, source_target_pairs={{0,16},{1,24},{2,18},{3,26},{4,20},{5,28},{6,22},{7,30},{8,0},{9,8... | collective-permute-start | bytes 1572872 | tf_op jit(solution)/shard_map/ppermute | solution.py:250
  386.4 45.5 %collective-permute-start.48 = (bf16[1024,256]{1,0:T(8,128)(2,1)}, bf16[1024,256]{1,0:T(8,128)(2,1)}, u32[]{:S(2)}, u32[]{:S(2)}) collective-permute-start(bf16[1024,256]{1,0:T(8,128)(2,1)} %get-tuple-element.81), channel_id=1, source_target_pairs={{0,24},{1,16},{2,26},{3,18},{4,28},{5,20},{6,30},{7,22},{8,8},{9,0... | collective-permute-start | bytes 1572872 | tf_op jit(solution)/shard_map/ppermute | solution.py:250
  388.4 51.9 %collective-permute-start.90 = (f32[256,256]{0,1:T(8,128)S(1)}, f32[256,256]{0,1:T(8,128)}, u32[]{:S(2)}, u32[]{:S(2)}) collective-permute-start(f32[256,256]{0,1:T(8,128)S(1)} %slice_bitcast_fusion.4), channel_id=1, source_target_pairs={{0,1},{1,0},{2,3},{3,2},{4,5},{5,4},{6,7},{7,6},{8,9},{9,8},{10,11... | collective-permute-start | bytes 786440 | tf_op jit(solution)/shard_map/ppermute | solution.py:250
  404.6 40.0 %collective-permute-start.75 = (bf16[256,1024]{0,1:T(8,128)(2,1)}, bf16[256,1024]{0,1:T(8,128)(2,1)}, u32[]{:S(2)}, u32[]{:S(2)}) collective-permute-start(bf16[256,1024]{0,1:T(8,128)(2,1)} %get-tuple-element.60), channel_id=1, source_target_pairs={{0,4},{1,5},{2,6},{3,7},{4,0},{5,1},{6,2},{7,3},{8,12},{9,13},{10,... | collective-permute-start | bytes 1572872 | tf_op jit(solution)/shard_map/ppermute | solution.py:250
  412.2 35.2 %collective-permute-start.72 = (bf16[256,1024]{0,1:T(8,128)(2,1)}, bf16[256,1024]{0,1:T(8,128)(2,1)}, u32[]{:S(2)}, u32[]{:S(2)}) collective-permute-start(bf16[256,1024]{0,1:T(8,128)(2,1)} %get-tuple-element.62), channel_id=1, source_target_pairs={{0,2},{1,3},{2,0},{3,1},{4,6},{5,7},{6,4},{7,5},{8,10},{9,11},{10,... | collective-permute-start | bytes 1572872 | tf_op jit(solution)/shard_map/ppermute | solution.py:250
  444.6 50.8 %collective-permute-start.66 = (bf16[1024,1024]{1,0:T(8,128)(2,1)}, bf16[1024,1024]{1,0:T(8,128)(2,1)}, u32[]{:S(2)}, u32[]{:S(2)}) collective-permute-start(bf16[1024,1024]{1,0:T(8,128)(2,1)} %get-tuple-element.40), channel_id=1, source_target_pairs={{0,1},{1,0},{2,3},{3,2},{4,5},{5,4},{6,7},{7,6},{8,9},{9,8},{10,11... | collective-permute-start | bytes 6291464 | tf_op jit(solution)/shard_map/ppermute | solution.py:250
  505.6 47.6 %collective-permute-start.68 = (bf16[1024,256]{1,0:T(8,128)(2,1)}, bf16[1024,256]{1,0:T(8,128)(2,1)S(1)}, u32[]{:S(2)}, u32[]{:S(2)}) collective-permute-start(bf16[1024,256]{1,0:T(8,128)(2,1)} %get-tuple-element.75), channel_id=1, source_target_pairs={{0,8},{1,0},{2,10},{3,2},{4,12},{5,4},{6,14},{7,6},{8,24},{9,16},{... | collective-permute-start | bytes 1572872 | tf_op jit(solution)/shard_map/ppermute | solution.py:250
  505.7 54.1 %collective-permute-start.69 = (bf16[1024,256]{1,0:T(8,128)(2,1)}, bf16[1024,256]{1,0:T(8,128)(2,1)S(1)}, u32[]{:S(2)}, u32[]{:S(2)}) collective-permute-start(bf16[1024,256]{1,0:T(8,128)(2,1)} %get-tuple-element.74), channel_id=1, source_target_pairs={{0,16},{1,24},{2,18},{3,26},{4,20},{5,28},{6,22},{7,30},{8,0},{9,8... | collective-permute-start | bytes 1572872 | tf_op jit(solution)/shard_map/ppermute | solution.py:250
  508.0 57.0 %collective-permute-start.70 = (bf16[1024,256]{1,0:T(8,128)(2,1)}, bf16[1024,256]{1,0:T(8,128)(2,1)S(1)}, u32[]{:S(2)}, u32[]{:S(2)}) collective-permute-start(bf16[1024,256]{1,0:T(8,128)(2,1)} %get-tuple-element.73), channel_id=1, source_target_pairs={{0,24},{1,16},{2,26},{3,18},{4,28},{5,20},{6,30},{7,22},{8,8},{9,0... | collective-permute-start | bytes 1572872 | tf_op jit(solution)/shard_map/ppermute | solution.py:250
  (102 other events, 1136.7 us)

commit v2 on v0

--- a/solution.py
+++ b/solution.py
@@ -1,6 +1,11 @@
+import functools
+
 import jax
 import jax.numpy as jnp
 from jax import lax
+from jax.experimental import pallas as pl
+from jax.experimental.pallas import tpu as pltpu
+from jax.sharding import Mesh
 from jax.sharding import PartitionSpec as P
 
 LENGTH = 1024
@@ -9,23 +14,613 @@
 eps_norm = 1e-05
 momentum = 0.1
 
+f32 = jnp.float32
+bf16 = jnp.bfloat16
+BIG = 56 * 2**20
+AXES = ("wide", "ring", "core")
+NARROW = ("ring", "core")
+
+
+def whole(space=pltpu.VMEM):
+    return pl.BlockSpec(memory_space=space)
+
+
+def stats_of(sums, count):
+    mean = sums[0] / count
+    var = sums[1] / count - mean * mean
+    return mean, var, lax.rsqrt(var + eps_norm)
+
+
+def tile_of(w, r, z, side, by_row):
+    return w[r, z, side] if by_row else w[z, r, side]
+
+
+def product_kernel(by_row, xs, xo, w, pre, sums):
+    blocks, rows, width = xs.shape
+    per = width // 128
+    parts = blocks * per
+
+    @pl.when(pl.program_id(0) == 0)
+    def _():
+        sums[...] = jnp.zeros_like(sums)
+
+    for z in range(blocks):
+        acc = None
+        for side, x in enumerate((xs, xo)):
+            for r in range(blocks):
+                term = jnp.dot(x[r], tile_of(w, r, z, side, by_row), preferred_element_type=f32)
+                acc = term if acc is None else acc + term
+        for k in range(per):
+            piece = acc[:, k * 128 : k * 128 + 128]
+            at = z * per + k
+            for g in range(rows // 8):
+                pre[pl.ds(g * 8 * parts + at, 8, stride=parts), :] = piece[g * 8 : g * 8 + 8]
+            sums[0, at : at + 1, :] += jnp.sum(piece, 0, keepdims=True)
+            sums[1, at : at + 1, :] += jnp.sum(piece * piece, 0, keepdims=True)
+
+
+def product(xs, xo, w, by_row, step=256):
+    blocks, rows, width = xs.shape
+    cols = blocks * width
+    parts = cols // 128
+    return pl.pallas_call(
+        functools.partial(product_kernel, by_row),
+        grid=(rows // step,),
+        in_specs=[
+            pl.BlockSpec((blocks, step, width), lambda i: (0, i, 0)),
+            pl.BlockSpec((blocks, step, width), lambda i: (0, i, 0)),
+            pl.BlockSpec(w.shape, lambda i: (0, 0, 0, 0, 0)),
+        ],
+        out_specs=[
+            pl.BlockSpec((step * parts, 128), lambda i: (i, 0)),
+            pl.BlockSpec((2, parts, 128), lambda i: (0, 0, 0)),
+        ],
+        out_shape=[
+            jax.ShapeDtypeStruct((rows * parts, 128), f32),
+            jax.ShapeDtypeStruct((2, parts, 128), f32),
+        ],
+        compiler_params=pltpu.CompilerParams(vmem_limit_bytes=BIG),
+        cost_estimate=pl.CostEstimate(flops=4 * rows * cols * cols, bytes_accessed=12 << 20, transcendentals=0),
+    )(xs, xo, w)
+
+
+def forward_kernel(count, sums, params, keep, pre, states, *rest):
+    ys, held = rest[:-1], rest[-1]
+    mean, _, rstd = stats_of(sums, count)
+    sc = params[0] * rstd
+    sh = params[1] - mean * sc
+    decay = params[2]
+    parts = sc.shape[0]
+    rows, width = ys[0].shape[1:]
+    per = width // 128
+    groups = rows // 16
+    block, blocks = pl.program_id(0), pl.num_programs(0)
+    first = block * rows
+
+    @pl.when(block == 0)
+    def _():
+        held[...] = jnp.zeros_like(held)
+
+    def scan(g, h):
+        for u in range(16):
+            t = g * 16 + u
+            at = pl.ds(pl.multiple_of(t * parts, parts), parts)
+            h = (decay * keep[first + t]) * h + (pre[at, :] * sc + sh)
+            states[at, :] = h
+        return h
+
+    def turn(y, g):
+        for k in range(parts):
+            two = []
+            for u in range(2):
+                h = states[pl.ds((g * 16 + u * 8) * parts + k, 8, stride=parts), :]
+                two.append(h / (1.0 + jnp.exp(-h)))
+            lane = k % per * 128
+            at = pl.ds(pl.multiple_of(g * 16, 16), 16)
+            y[k // per, at, lane : lane + 128] = jnp.concatenate(two, 0).astype(bf16)
+
+    def run(y):
+        def both(g, h):
+            turn(y, g - 1)
+            return scan(g, h)
+
+        held[...] = lax.fori_loop(1, groups, both, scan(0, held[...]))
+        turn(y, groups - 1)
+
+    for n, y in enumerate(ys):
+        pl.when(block // (blocks // len(ys)) == n)(functools.partial(run, y))
+
+
+def forward(sums, params, keep, pre, count, blocks, pieces, step=512):
+    parts = params.shape[1]
+    rows = pre.shape[0] // parts
+    each = rows // pieces // step
+    width = parts * 128 // blocks
+
+    def piece(n):
+        return pl.BlockSpec((blocks, step, width), lambda i: (0, jnp.clip(i - n * each, 0, each - 1), 0))
+
+    return pl.pallas_call(
+        functools.partial(forward_kernel, count),
+        grid=(rows // step,),
+        in_specs=[
+            pl.BlockSpec(sums.shape, lambda i: (0, 0, 0)),
+            pl.BlockSpec(params.shape, lambda i: (0, 0, 0)),
+            whole(pltpu.SMEM),
+            pl.BlockSpec((step * parts, 128), lambda i: (i, 0)),
+        ],
+        out_specs=[pl.BlockSpec((step * parts, 128), lambda i: (i, 0))] + [piece(n) for n in range(pieces)],
+        out_shape=[jax.ShapeDtypeStruct(pre.shape, f32)]
+        + [jax.ShapeDtypeStruct((blocks, rows // pieces, width), bf16)] * pieces,
+        scratch_shapes=[pltpu.VMEM((parts, 128), f32)],
+        compiler_params=pltpu.CompilerParams(vmem_limit_bytes=BIG),
+        cost_estimate=pl.CostEstimate(flops=12 * pre.size, bytes_accessed=10 * pre.size, transcendentals=pre.size),
+    )(sums, params, keep, pre)
+
+
+def backward_kernel(count, terms, sums, params, keep, pre, states, before, *rest):
+    dys, (carried, totals, slots, held) = rest[:-4], rest[-4:]
+    mean, _, rstd = stats_of(sums, count)
+    shift = -mean * rstd
+    decay = params[2]
+    parts = decay.shape[0]
+    rows, width = dys[0].shape[1:]
+    groups = rows // 16
+    per = width // 128
+    pieces = [dys[n : n + terms] for n in range(0, len(dys), terms)]
+    blocks = pl.num_programs(0)
+    block = blocks - 1 - pl.program_id(0)
+    first = block * rows
+
+    @pl.when(pl.program_id(0) == 0)
+    def _():
+        held[...] = jnp.zeros_like(held)
+
+    def turn(g, slot):
+        at = pl.ds(pl.multiple_of(g * 16, 16), 16)
+        for k in range(parts):
+            lane = k % per * 128
+            value = None
+            for n, piece in enumerate(pieces):
+                v = piece[0][k // per, at, lane : lane + 128].astype(f32)
+                for d in piece[1:]:
+                    v = v + d[k // per, at, lane : lane + 128].astype(f32)
+                value = v if value is None else jnp.where(block >= n * (blocks // len(pieces)), v, value)
+            for u in range(2):
+                slots[slot, pl.ds(u * 8 * parts + k, 8, stride=parts), :] = value[u * 8 : u * 8 + 8]
+
+    def scan(g, slot, carry, begin=None):
+        for u in range(15, -1, -1):
+            back, sg, sx, sd = carry
+            t = g * 16 + u
+            at = pl.ds(pl.multiple_of(t * parts, parts), parts)
+            h = states[at, :]
+            s = 1.0 / (1.0 + jnp.exp(-h))
+            dy = slots[slot, u * parts : u * parts + parts, :]
+            value = dy * (s + h * s * (1.0 - s)) + back
+            carried[at, :] = value
+            k = keep[first + t]
+            if begin is not None and u == 0:
+                prior = begin
+            else:
+                prior = states[pl.ds(pl.multiple_of((t - 1) * parts, parts), parts), :]
+            carry = (
+                (decay * k) * value,
+                sg + value,
+                sx + value * (pre[at, :] * rstd + shift),
+                sd + (value * k) * prior,
+            )
+        return carry
+
+    def two(i, carry):
+        g = groups - 1 - 2 * i
+        turn(g - 1, 1)
+        carry = scan(g, 0, carry)
+        turn(g - 2, 0)
+        return scan(g - 1, 1, carry)
+
+    turn(groups - 1, 0)
+    carry = lax.fori_loop(0, groups // 2 - 1, two, (held[0], held[1], held[2], held[3]))
+    turn(0, 1)
+    carry = scan(1, 0, carry)
+    begin = jnp.where(block == 0, jnp.zeros_like(decay), before[...])
+    carry = scan(0, 1, carry, begin)
+    for n in range(4):
+        held[n] = carry[n]
+    totals[0], totals[1], totals[2] = carry[1], carry[2], carry[3]
+
+
+def backward(sums, params, keep, pre, states, dys, terms, count, step=256):
+    parts = params.shape[1]
+    rows = pre.shape[0] // parts
+    last = rows // step - 1
+    blocks, _, width = dys[0].shape
+    pieces = len(dys) // terms
+    each = rows // pieces // step
+
+    def piece(n):
+        return pl.BlockSpec((blocks, step, width), lambda i: (0, jnp.clip(last - i - n * each, 0, each - 1), 0))
+
+    long = pl.BlockSpec((step * parts, 128), lambda i: (last - i, 0))
+    return pl.pallas_call(
+        functools.partial(backward_kernel, count, terms),
+        grid=(rows // step,),
+        in_specs=[
+            pl.BlockSpec(sums.shape, lambda i: (0, 0, 0)),
+            pl.BlockSpec(params.shape, lambda i: (0, 0, 0)),
+            whole(pltpu.SMEM),
+            long,
+            long,
+            pl.BlockSpec((parts, 128), lambda i: (jnp.maximum((last - i) * step - 1, 0), 0)),
+        ]
+        + [piece(n // terms) for n in range(len(dys))],
+        out_specs=[long, pl.BlockSpec((3, parts, 128), lambda i: (0, 0, 0))],
+        out_shape=[
+            jax.ShapeDtypeStruct(pre.shape, f32),
+            jax.ShapeDtypeStruct((3, parts, 128), f32),
+        ],
+        scratch_shapes=[pltpu.VMEM((2, 16 * parts, 128), f32), pltpu.VMEM((4, parts, 128), f32)],
+        compiler_params=pltpu.CompilerParams(vmem_limit_bytes=BIG),
+        cost_estimate=pl.CostEstimate(flops=24 * pre.size, bytes_accessed=16 * pre.size, transcendentals=pre.size),
+    )(sums, params, keep, pre, states, states, *dys)
+
+
+def times_side(d, w, out, by_row, side=0):
+    dims = (((1,), (1,)), ((), ()))
+    blocks, _, width = out.shape
+    for r in range(blocks):
+        acc = None
+        for z in range(blocks):
+            piece = d[:, z * width : z * width + width]
+            term = lax.dot_general(piece, tile_of(w, r, z, side, by_row), dims, preferred_element_type=f32)
+            acc = term if acc is None else acc + term
+        out[r] = acc.astype(out.dtype)
+
+
+def side_of(w, side):
+    return pl.BlockSpec(w.shape[:2] + (1,) + w.shape[3:], lambda i: (0, 0, side, 0, 0))
+
+
+def spread_kernel(count, by_row, sums, params, totals, carried, pre, w, dpre, *outs):
+    mean, _, rstd = stats_of(sums, count)
+    sc = params[0] * rstd
+    slope = sc * rstd * (totals[1] / count)
+    c3 = mean * slope - sc * (totals[0] / count)
+    parts = sc.shape[0]
+    for g in range(dpre.shape[0] // 16):
+        for k in range(parts):
+            both = []
+            for u in range(2):
+                at = pl.ds((g * 16 + u * 8) * parts + k, 8, stride=parts)
+                both.append(sc[k : k + 1] * carried[at, :] - slope[k : k + 1] * pre[at, :] + c3[k : k + 1])
+            dpre[g * 16 : g * 16 + 16, k * 128 : k * 128 + 128] = jnp.concatenate(both, 0).astype(bf16)
+    for side, out in enumerate(outs):
+        times_side(dpre, w, out, by_row, side)
+
+
+def spread(sums, params, totals, carried, pre, w, by_row, count, sides, step=512):
+    parts = params.shape[1]
+    rows, cols = pre.shape[0] // parts, parts * 128
+    blocks, width = w.shape[0], w.shape[4]
+    return pl.pallas_call(
+        functools.partial(spread_kernel, count, by_row),
+        grid=(rows // step,),
+        in_specs=[
+            pl.BlockSpec(sums.shape, lambda i: (0, 0, 0)),
+            pl.BlockSpec(params.shape, lambda i: (0, 0, 0)),
+            pl.BlockSpec(totals.shape, lambda i: (0, 0, 0)),
+            pl.BlockSpec((step * parts, 128), lambda i: (i, 0)),
+            pl.BlockSpec((step * parts, 128), lambda i: (i, 0)),
+            side_of(w, 1) if sides == 1 else pl.BlockSpec(w.shape, lambda i: (0, 0, 0, 0, 0)),
+        ],
+        out_specs=[pl.BlockSpec((step, cols), lambda i: (i, 0))]
+        + [pl.BlockSpec((blocks, step, width), lambda i: (0, i, 0))] * sides,
+        out_shape=[jax.ShapeDtypeStruct((rows, cols), bf16)]
+        + [jax.ShapeDtypeStruct((blocks, rows, width), bf16)] * sides,
+        compiler_params=pltpu.CompilerParams(vmem_limit_bytes=BIG),
+        cost_estimate=pl.CostEstimate(flops=2 * sides * rows * cols * cols, bytes_accessed=16 << 20, transcendentals=0),
+    )(sums, params, totals, carried, pre, w)
+
+
+def spread_own_kernel(by_row, dpre, w, same):
+    times_side(dpre, w, same, by_row)
+
+
+def spread_own(dpre, w, by_row, step=512):
+    rows, cols = dpre.shape
+    blocks, width = w.shape[0], w.shape[4]
+    return pl.pallas_call(
+        functools.partial(spread_own_kernel, by_row),
+        grid=(rows // step,),
+        in_specs=[pl.BlockSpec((step, cols), lambda i: (i, 0)), side_of(w, 0)],
+        out_specs=pl.BlockSpec((blocks, step, width), lambda i: (0, i, 0)),
+        out_shape=jax.ShapeDtypeStruct((blocks, rows, width), bf16),
+        compiler_params=pltpu.CompilerParams(vmem_limit_bytes=BIG),
+        cost_estimate=pl.CostEstimate(flops=2 * rows * cols * cols, bytes_accessed=6 << 20, transcendentals=0),
+    )(dpre, w)
+
+
+def load_kernel(same, other, late, out):
+    rows = same.shape[1]
+    out[0, :rows, :] = (same[0].astype(f32) + other[0].astype(f32)).astype(out.dtype)
+    out[0, rows:, :] = late[0]
+
+
+def load(same, other, late):
+    blocks, rows, width = same.shape
+    more = late.shape[1]
+    return pl.pallas_call(
+        load_kernel,
+        grid=(blocks,),
+        in_specs=[
+            pl.BlockSpec((1, rows, width), lambda i: (i, 0, 0)),
+            pl.BlockSpec((1, rows, width), lambda i: (i, 0, 0)),
+            pl.BlockSpec((1, more, width), lambda i: (i, 0, 0)),
+        ],
+        out_specs=pl.BlockSpec((1, rows + more, width), lambda i: (i, 0, 0)),
+        out_shape=jax.ShapeDtypeStruct((blocks, rows + more, width), bf16),
+        compiler_params=pltpu.CompilerParams(vmem_limit_bytes=BIG),
+        cost_estimate=pl.CostEstimate(flops=0, bytes_accessed=8 << 20, transcendentals=0),
+    )(same, other, late)
+
+
+def outer_kernel(by_row, xs, xo, dpre, out):
+    width = xs.shape[2]
+    dims = (((0,), (0,)), ((), ()))
+    for side, x in enumerate((xs, xo)):
+        term = lax.dot_general(x[0], dpre[...], dims, preferred_element_type=f32).astype(bf16)
+        for z in range(dpre.shape[1] // width):
+            piece = term[:, z * width : z * width + width]
+            if by_row:
+                out[0, z, side] = piece
+            else:
+                out[z, 0, side] = piece
+
+
+def outer(xs, xo, dpre, by_row):
+    blocks, rows, width = xs.shape
+    tile = (1, blocks, 2, width, width) if by_row else (blocks, 1, 2, width, width)
+    return pl.pallas_call(
+        functools.partial(outer_kernel, by_row),
+        grid=(blocks,),
+        in_specs=[
+            pl.BlockSpec((1, rows, width), lambda i: (i, 0, 0)),
+            pl.BlockSpec((1, rows, width), lambda i: (i, 0, 0)),
+            pl.BlockSpec(dpre.shape, lambda i: (0, 0)),
+        ],
+        out_specs=pl.BlockSpec(tile, (lambda i: (i, 0, 0, 0, 0)) if by_row else (lambda i: (0, i, 0, 0, 0))),
+        out_shape=jax.ShapeDtypeStruct((blocks, blocks, 2, width, width), bf16),
+        compiler_params=pltpu.CompilerParams(vmem_limit_bytes=BIG),
+        cost_estimate=pl.CostEstimate(flops=4 * rows * dpre.shape[1] ** 2, bytes_accessed=10 << 20, transcendentals=0),
+    )(xs, xo, dpre)
+
+
+def place_kernel(core, mine, theirs, *rest):
+    out = rest[-1]
+    half = out.shape[1] // 2
+    c = core[0]
+    out[:, pl.ds(pl.multiple_of(c * half, half), half)] = mine[0].astype(out.dtype)
+    out[:, pl.ds(pl.multiple_of((1 - c) * half, half), half)] = theirs[0].astype(out.dtype)
+
+
+def place(core, mine, theirs, kind, piece, pieces, before):
+    count, length, half = theirs.shape
+    spec = pl.BlockSpec((length, 2 * half), lambda i, core: (i * pieces + piece, 0))
+    prior = [] if before is None else [before]
+    return pl.pallas_call(
+        place_kernel,
+        grid_spec=pltpu.PrefetchScalarGridSpec(
+            num_scalar_prefetch=1,
+            grid=(count,),
+            in_specs=[
+                pl.BlockSpec((1, length, half), lambda i, core: (core[0] * count + i, 0, 0)),
+                pl.BlockSpec((1, length, half), lambda i, core: (i, 0, 0)),
+            ]
+            + [pl.BlockSpec(memory_space=pl.ANY)] * len(prior),
+            out_specs=spec,
+        ),
+        out_shape=jax.ShapeDtypeStruct((count * length * pieces, 2 * half), kind),
+        input_output_aliases={3: 0} if prior else {},
+        compiler_params=pltpu.CompilerParams(vmem_limit_bytes=BIG),
+        cost_estimate=pl.CostEstimate(flops=0, bytes_accessed=6 << 20, transcendentals=0),
+    )(core, mine, theirs, *prior)
+
+
+def paired(frames, weights, gains, shifts, decays, resets, running, grad_out):
+    wide, narrow = lax.axis_size("wide"), lax.axis_size(NARROW)
+    rows, lanes = frames.shape
+    half = lanes // 2
+    depth = weights.shape[1]
+    count = rows * narrow * 1.0
+    z = lax.axis_index("wide")
+    r, c = lax.axis_index("ring"), lax.axis_index("core")
+
+    def send(x, to):
+        pairs = []
+        for a in range(wide):
+            for b in range(narrow):
+                tz, tr, tc = to(a, b // 2, b % 2)
+                pairs.append((a * narrow + b, tz * narrow + tr * 2 + tc))
+        return lax.ppermute(x, AXES, pairs)
+
+    def swap(x):
+        return send(x, lambda a, b, d: (a, b, 1 - d))
+
+    def over_ring(x, m):
+        return send(x, lambda a, b, d: (a, b ^ m, d))
+
+    def over_wide(x, m):
+        return send(x, lambda a, b, d: (a ^ m, b, d))
+
+    def everywhere(x, extra=None):
+        a1, a2, a3 = over_ring(x, 1), over_ring(x, 2), over_ring(x, 3)
+        x = (x + a1) + (a2 + a3)
+        if extra is None:
+            a1, a2, a3 = over_wide(x, 1), over_wide(x, 2), over_wide(x, 3)
+            return (x + a1) + (a2 + a3)
+        load = jnp.concatenate([x.reshape(-1, 128), extra])
+        got = [over_wide(load, m) for m in range(1, wide)]
+        a1, a2, a3 = (g[: x.size // 128].reshape(x.shape) for g in got)
+        return (x + a1) + (a2 + a3), [extra] + [g[x.size // 128 :] for g in got]
+
+    def placed(pieces, shape, spots):
+        buf = jnp.zeros(shape, pieces[0].dtype)
+        for piece, spot in zip(pieces, spots, strict=True):
+            buf = lax.dynamic_update_slice(buf, piece, spot)
+        return buf
+
+    def by_half(x, first, length):
+        x = x.reshape(wide // 2, LENGTH, lanes)[:, first : first + length]
+        mine = lax.dynamic_slice(x, (0, 0, c * half), (wide // 2, length, half))
+        theirs = swap(lax.dynamic_slice(x, (0, 0, (1 - c) * half), (wide // 2, length, half)))
+        return jnp.concatenate([jnp.where(c == 0, mine, theirs), jnp.where(c == 0, theirs, mine)])
+
+    def exchange(x):
+        return lax.all_to_all(x, "wide", 0, 0, tiled=True)
+
+    def others(mine):
+        return swap(lax.dynamic_slice_in_dim(mine, (1 - c) * (wide // 2), wide // 2, 0))
+
+    def halves(w):
+        axis = w.ndim - 1
+        own = lax.dynamic_slice_in_dim(w, c * half, half, axis)
+        return own, swap(lax.dynamic_slice_in_dim(w, (1 - c) * half, half, axis))
+
+    def along_ring(line):
+        pieces = [line] + [over_ring(line, m) for m in range(1, 4)]
+        return placed([p[None] for p in pieces], (4,) + line.shape, [(r ^ m,) + (0,) * line.ndim for m in range(4)])
+
+    def gathered_late(both):
+        return lax.all_gather(lax.all_gather(both, "wide"), "ring")
+
+    def ring_pieces(tiles):
+        pieces = [lax.dynamic_index_in_dim(tiles, r ^ m, 0, keepdims=False) for m in range(4)]
+        return pieces[:1] + [over_ring(pieces[m], m) for m in range(1, 4)]
+
+    def rows_late(tiles):
+        return lax.psum_scatter(tiles.reshape(4 * wide * 2, depth, half), "ring", scatter_dimension=0, tiled=True)
+
+    theirs = swap(resets)
+    row = jnp.where(c == z // 2, resets, theirs)
+    keep = 1.0 - lax.dynamic_slice(row, ((z % 2) * LENGTH,), (LENGTH,)).astype(f32)
+    vectors = jnp.concatenate([gains, shifts, decays])
+    vectors = lax.dynamic_slice(vectors, (0, c * half), (6, half)).reshape(-1, 128)
+
+    second = jnp.stack(halves(weights[1]))
+    shards = [weights[0]] + [over_wide(weights[0], m) for m in range(1, wide)]
+    x = by_half(frames, 0, LENGTH)
+    cut = LENGTH // 2
+    x, shards, keep, grad_out, second = lax.optimization_barrier((x, shards, keep, grad_out, second))
+    mats = [None, gathered_late(second)]
+    xs = exchange(x)
+    line = jnp.stack(halves(jnp.stack(shards)), 1)
+    line = placed([line[m][None] for m in range(wide)], line.shape, [(z ^ m, 0, 0, 0) for m in range(wide)])
+    mats[0] = along_ring(line)
+    g_early, g_late = by_half(grad_out, 0, cut), by_half(grad_out, cut, cut)
+    xs, mats[0], g_late = lax.optimization_barrier((xs, mats[0], g_late))
+    xo = swap(xs)
+    g_late = exchange(g_late)
+
+    saved = []
+    ins = (xs, xo)
+    for level in range(2):
+        pre, sums = product(*ins, mats[level], True)
+        if level == 0:
+            sums, pieces = everywhere(sums, vectors)
+            spots = [(0, (z ^ m) * half) for m in range(wide)]
+            vectors = placed([p.reshape(6, half) for p in pieces], (6, wide * half), spots)
+            vectors = vectors.reshape(3, 2, -1, 128)
+            params = [vectors[:, i] for i in range(2)]
+            sums, g_late, g_early = lax.optimization_barrier((sums, g_late, g_early))
+            g_early = exchange(g_early)
+        else:
+            sums = everywhere(sums)
+        states, *y = forward(sums, params[level], keep, pre, count, wide, 1 + level)
+        saved.append((ins, pre, sums, states))
+        if level == 0:
+            ins = (y[0], swap(y[0]))
+    out_early = exchange(y[0])
+
+    core = c.reshape(1)
+    dys, terms = (g_early, g_late), 1
+    totals_list = [None, None]
+    for level in (1, 0):
+        ins, pre, sums, states = saved[level]
+        carried, totals = backward(sums, params[level], keep, pre, states, dys, terms, count)
+        totals = everywhere(totals)
+        totals_list[level] = totals
+        if level:
+            out_early, out_late, totals = lax.optimization_barrier((out_early, y[1], totals))
+            out_late = exchange(out_late)
+        else:
+            out_early, out_late, totals = lax.optimization_barrier((out_early, out_late, totals))
+        back_of = functools.partial(spread, sums, params[level], totals, carried, pre, mats[level], True, count)
+        if level:
+            dpre, other = back_of(1)
+            other = swap(other)
+            tiles = outer(*ins, dpre, True)
+            tiles, dpre = lax.optimization_barrier((tiles, dpre))
+            late = rows_late(tiles)
+            dys, terms = (spread_own(dpre, mats[level], True), other), 2
+        else:
+            dpre, other = back_of(1)
+            other = swap(other)
+            same = spread_own(dpre, mats[level], True)
+            both = exchange(load(same, other, late.reshape(wide, 2 * depth, half)))
+            tiles = outer(*ins, dpre, True)
+            sent = place(core, out_early, others(out_early), bf16, 0, 2, None)
+            sent = place(core, out_late, others(out_late), bf16, 1, 2, sent)
+            pieces, sent = lax.optimization_barrier((ring_pieces(tiles), sent))
+            pieces = [p.astype(f32) for p in pieces]
+            line = ((pieces[0] + pieces[1]) + (pieces[2] + pieces[3])).astype(bf16)
+            own, away = line[:, 0], swap(line[:, 1])
+            line = jnp.concatenate([jnp.where(c == 0, own, away), jnp.where(c == 0, away, own)], axis=2)
+            line, both = lax.optimization_barrier((line, both))
+            line = exchange(line)
+            back = place(core, both, others(both[:, :LENGTH]), f32, 0, 1, None)
+            late = jnp.sum(both[:, LENGTH:].astype(f32), 0).reshape(2, depth, half)
+            own, away = late[0], swap(late[1])
+            late = jnp.concatenate([jnp.where(c == 0, own, away), jnp.where(c == 0, away, own)], axis=1)
+            line, back, late = lax.optimization_barrier((line, back, late))
+            weight_grad = jnp.stack([jnp.sum(line.astype(f32), 0), late])
+
+    small = []
+    for level in range(2):
+        mean, var, _ = stats_of(saved[level][2], count)
+        small.append(jnp.concatenate([mean[None], var[None], totals_list[level]]))
+    small = jnp.stack(small).reshape(2, 5, wide, half)
+    small = lax.dynamic_index_in_dim(small, z, 2, keepdims=False)
+    away = swap(small)
+    small = jnp.concatenate([jnp.where(c == 0, small, away), jnp.where(c == 0, away, small)], axis=2)
+    new_mean = (1.0 - momentum) * running[:, 0] + momentum * small[:, 0]
+    new_var = (1.0 - momentum) * running[:, 1] + momentum * small[:, 1] * count / (count - 1.0)
+    return (
+        sent,
+        back,
+        weight_grad,
+        small[:, 3],
+        small[:, 2],
+        small[:, 4],
+        jnp.stack([new_mean, new_var], axis=1),
+    )
+
 
 def link(earlier, later):
     return (earlier[0] * later[0], later[0] * earlier[1] + later[1])
 
 
-def per_device(frames, weights, gains, shifts, decays, resets, running, grad_out):
+def general(frames, weights, gains, shifts, decays, resets, running, grad_out):
     frame_rows, lanes = frames.shape
-    count = frame_rows * lax.axis_size("narrow") * 1.0
+    count = frame_rows * lax.axis_size(NARROW) * 1.0
     keep = (1 - resets).astype(jnp.float32).reshape(-1, LENGTH, 1)
     layer_in = frames
     saved = []
     updated = []
     for level in range(2):
         full_in = lax.all_gather(layer_in, "wide", axis=1, tiled=True)
-        full_weight = lax.all_gather(weights[level], "narrow", axis=0, tiled=True)
+        full_weight = lax.all_gather(weights[level], NARROW, axis=0, tiled=True)
         pre = jnp.dot(full_in, full_weight, preferred_element_type=jnp.float32)
-        total, squares = lax.psum((jnp.sum(pre, 0), jnp.sum(pre * pre, 0)), "narrow")
+        total, squares = lax.psum((jnp.sum(pre, 0), jnp.sum(pre * pre, 0)), NARROW)
         mean = total / count
         var = squares / count - mean * mean
         scale = lax.rsqrt(var + eps_norm)
@@ -54,7 +649,7 @@
         decay_term = jnp.sum(carried * keep * prior, axis=(0, 1))
         carried = carried.reshape(frame_rows, lanes)
         shift_sum, gain_sum, decay_sum = lax.psum(
-            (jnp.sum(carried, 0), jnp.sum(carried * normed_hat, 0), decay_term), "narrow"
+            (jnp.sum(carried, 0), jnp.sum(carried * normed_hat, 0), decay_term), NARROW
         )
         grad_pre = (
             gains[level] * scale * (carried - shift_sum / count - normed_hat * gain_sum / count)
@@ -63,7 +658,7 @@
             lax.dot_general(
                 full_in, grad_pre, (((0,), (0,)), ((), ())), preferred_element_type=jnp.float32
             ),
-            "narrow",
+            NARROW,
             scatter_dimension=0,
             tiled=True,
         )
@@ -85,25 +680,37 @@
     )
 
 
+def per_device(frames, weights, *rest):
+    wide, narrow = lax.axis_size("wide"), lax.axis_size(NARROW)
+    rows, lanes = frames.shape
+    one_row_a_chip = 2 * rows == wide * LENGTH and wide == 4 and narrow == 2 * wide
+    if one_row_a_chip and lanes == 2 * weights.shape[1] and wide * lanes == 2048:
+        return paired(frames, weights, *rest)
+    return general(frames, weights, *rest)
+
+
 def solution(mesh):
+    wide, narrow = mesh.shape["wide"], mesh.shape["narrow"]
+    devices = mesh.devices if mesh.axis_names == ("wide", "narrow") else mesh.devices.T
+    cut = Mesh(devices.reshape(wide, narrow // 2, 2), AXES)
     placed = (
-        P("narrow", "wide"),
-        P(None, "narrow", "wide"),
+        P(NARROW, "wide"),
+        P(None, NARROW, "wide"),
         P(None, "wide"),
         P(None, "wide"),
         P(None, "wide"),
-        P("narrow"),
+        P(NARROW),
         P(None, None, "wide"),
-        P("narrow", "wide"),
+        P(NARROW, "wide"),
     )
     return jax.shard_map(
         per_device,
-        mesh=mesh,
+        mesh=cut,
         in_specs=placed,
         out_specs=(
-            P("narrow", "wide"),
-            P("narrow", "wide"),
-            P(None, "narrow", "wide"),
+            P(NARROW, "wide"),
+            P(NARROW, "wide"),
+            P(None, NARROW, "wide"),
             P(None, "wide"),
             P(None, "wide"),
             P(None, "wide"),

time: 1870 us -> 409 us (0.22); the launches traced: 1840 us -> 403 us
  local copies, waits for them, and re-layouts: 851 us -> 29.5 us
  waiting for transfers between devices: 661 us -> 148 us
  other arithmetic: 204 us -> 21.8 us
  Pallas kernels: 0 us -> 104 us
  starting transfers between devices: 0.32 us -> 85.6 us
  matrix products: 59.5 us -> 0 us
  blocking collectives: 51.4 us -> 0 us
    slice x258 -> x8, local copies, waits for them, and re-layouts: 660 us -> 1.37 us  [the longest x1 1.06 us: paired(): second = jnp.stack(halves(weights[1]))]
    reduce_scatter x4 -> x1, waiting for transfers between devices: 495 us -> 4.1 us  [rows_late(): lax.psum_scatter(tiles.reshape(4 * wide * 2, depth, half), 'ring', scatte...]
    all_gather x4 -> x2, waiting for transfers between devices: 164 us -> 49.5 us  [gathered_late(): return lax.all_gather(lax.all_gather(both, 'wide'), 'ring')]
    pallas_call x0 -> x16, Pallas kernels: none -> 104 us  [the longest x2 18.5 us: product(): pl.pallas_call(functools.partial(product_kernel, by_row), grid=(rows // s...]
    pad x72 -> x0, local copies, waits for them, and re-layouts: 101 us -> none  [the longest x36 51 us: per_device(): lax.associative_scan(link, (rate_next, grad_state), reverse=True, axis=1)]
    add x81 -> x9, other arithmetic: 85.9 us -> 5.85 us  [the longest x4 2.83 us: everywhere(): x = x + a1 + (a2 + a3)]
    ppermute x0 -> x49, waiting for transfers between devices: none -> 77.3 us  [send(): return lax.ppermute(x, AXES, pairs)]
    mul x36 -> x0, other arithmetic: 65.8 us -> none  [the longest x32 52.7 us: link(): return (earlier[0] * later[0], later[0] * earlier[1] + later[1])]
  transfers between devices with their start and end apart: 8 -> 59, of which waited for: 5 -> 36; matrix products, arithmetic and copies ran while one was open for 37% -> 11% of each run, Pallas kernels for 0% -> 21%
where the time goes in v2:
time: 409 us; the launch traced here: 403 us
  waiting for transfers between devices  148 us (36%)
  Pallas kernels  104 us (25%)
  starting transfers between devices  85.6 us (21%)
  local copies, waits for them, and re-layouts  29.5 us (7%)
  other arithmetic  21.8 us (5%)
  between operations  14.3 us (3%)
    ppermute x49, waiting for transfers between devices, send(): return lax.ppermute(x, AXES, pairs)  77.3 us
    all_gather x2, waiting for transfers between devices, gathered_late(): return lax.all_gather(lax.all_gather(both, 'wide'), 'ring')  49.5 us
    all_to_all x7, starting transfers between devices, exchange(): return lax.all_to_all(x, 'wide', 0, 0, tiled=True)  42.8 us
    ppermute x49, starting transfers between devices, send(): return lax.ppermute(x, AXES, pairs)  42.8 us
    pallas_call x2, Pallas kernels, product(): pl.pallas_call(functools.partial(product_kernel, by_row), grid=(rows // s...  18.5 us
    all_to_all x7, waiting for transfers between devices, exchange(): return lax.all_to_all(x, 'wide', 0, 0, tiled=True)  17.3 us
    pallas_call x2, Pallas kernels, backward(): pl.pallas_call(functools.partial(backward_kernel, count, terms), grid=(ro...  17.3 us
    pallas_call x2, Pallas kernels, outer(): pl.pallas_call(functools.partial(outer_kernel, by_row), grid=(blocks,), i...  16.9 us
  transfers between devices with their start and end apart: 59, of which 36 were waited for; matrix products, arithmetic and copies ran while one was open for 11% of the time, Pallas kernels for 21%

profile of v2, /device:TPU:28, one launch (start us, length us, event | category | flops | bytes accessed | tf_op | source)
XLA Modules:
  0.0 403.4 jit_solution(2557519717786663281)
XLA Ops:
  25.1 8.7 %collective-permute-done.2 = bf16[256,512]{1,0:T(8,128)(2,1)} collective-permute-done((bf16[256,512]{1,0:T(8,128)(2,1)S(1)}, bf16[256,512]{1,0:T(8,128)(2,1)}, u32[]{:S(2)}, u32[]{:S(2)}) %collective-permute-start.2) | collective-permute-done | bytes 262176 | tf_op jit(solution)/shard_map/ppermute | solution.py:444
  33.8 9.1 %all-to-all-start = ((bf16[4,1024,256]{2,1,0:T(8,128)(2,1)}), bf16[4,1024,256]{2,1,0:T(8,128)(2,1)}, u32[]{:S(2)}, u32[]{:S(2)}) async-start(bf16[4,1024,256]{2,1,0:T(8,128)(2,1)} %pad_maximum_fusion), calls=%async_computation | async-start | bytes 4194304 | tf_op jit(solution)/shard_map/all_to_all | solution.py:479
  57.8 44.9 %all-gather.5.cloned.1.call-done = bf16[8,256,256]{2,1,0:T(8,128)(2,1)} async-done(((bf16[2,256,256]{2,1,0:T(8,128)(2,1)}), bf16[8,256,256]{2,1,0:T(8,128)(2,1)}) %all-gather.5.cloned.1.call-update) | async-done | bytes 1048592 | tf_op jit(solution)/shard_map/all_gather | solution.py:494
  109.5 5.1 %all-to-all-start.1 = ((bf16[4,512,256]{2,1,0:T(8,128)(2,1)}), bf16[4,512,256]{2,1,0:T(8,128)(2,1)S(1)}, u32[]{:S(2)}, u32[]{:S(2)}) async-start(bf16[4,512,256]{2,1,0:T(8,128)(2,1)} %pad_maximum_fusion.2), calls=%async_computation.1 | async-start | bytes 2097152 | tf_op jit(solution)/shard_map/all_to_all | solution.py:479
  114.6 9.4 %shard_map.135 = (f32[8192,128]{1,0:T(8,128)}, f32[2,8,128]{2,1,0:T(8,128)}) custom-call(bf16[4,1024,256]{2,1,0:T(8,128)(2,1)} %all-to-all-done.xs, bf16[4,1024,256]{2,1,0:T(8,128)(2,1)} %collective-permute-done.11.xo, bf16[4,4,2,256,256]{4,3,2,1,0:T(8,128)(2,1)} %bitcast_dynamic-update-slice_fusion.w), custom_call_target="tpu_custom_call" | custom-call | flops 4294967296 | bytes 12582912 | tf_op jit(solution)/shard_map/pallas_call | solution.py:66
  141.5 6.2 %shard_map.136 = (f32[8192,128]{1,0:T(8,128)}, bf16[4,1024,256]{2,1,0:T(8,128)(2,1)}) custom-call(f32[2,8,128]{2,1,0:T(8,128)} %fusion.12.sums, f32[3,8,128]{2,1,0:T(8,128)} %get-tuple-element.144.params, f32[1024]{0:T(1024)} %fusion.22.keep, f32[8192,128]{1,0:T(8,128)} %get-tuple-element.68.pre), custom_call_target="tpu_custom_call" | custom-call | flops 12582912 | bytes 10485760 | tf_op jit(solution)/shard_map/pallas_call | solution.py:143
  147.7 5.9 %all-to-all-start.3 = ((bf16[4,512,256]{2,1,0:T(8,128)(2,1)}), bf16[4,512,256]{2,1,0:T(8,128)(2,1)S(1)}, u32[]{:S(2)}, u32[]{:S(2)}) async-start(bf16[4,512,256]{2,1,0:T(8,128)(2,1)} %pad_maximum_fusion.3), calls=%async_computation.3 | async-start | bytes 2097152 | tf_op jit(solution)/shard_map/all_to_all | solution.py:479
  158.2 9.2 %shard_map.137 = (f32[8192,128]{1,0:T(8,128)}, f32[2,8,128]{2,1,0:T(8,128)}) custom-call(bf16[4,1024,256]{2,1,0:T(8,128)(2,1)} %get-tuple-element.69.xs, bf16[4,1024,256]{2,1,0:T(8,128)(2,1)} %collective-permute-done.19.xo, bf16[4,4,2,256,256]{4,3,2,1,0:T(8,128)(2,1)} %bitcast.77), custom_call_target="tpu_custom_call" | custom-call | flops 4294967296 | bytes 12582912 | tf_op jit(solution)/shard_map/pallas_call | solution.py:66
  181.1 6.5 %shard_map.138 = (f32[8192,128]{1,0:T(8,128)}, bf16[4,512,256]{2,1,0:T(8,128)(2,1)}, bf16[4,512,256]{2,1,0:T(8,128)(2,1)}) custom-call(f32[2,8,128]{2,1,0:T(8,128)} %add_add_fusion.4.sums, f32[3,8,128]{2,1,0:T(8,128)} %get-tuple-element.143.params, f32[1024]{0:T(1024)} %fusion.22.keep, f32[8192,128]{1,0:T(8,128)} %get-tuple-element.72.pre), custom_call_target="tpu_custom_call" | custom-call | flops 12582912 | bytes 10485760 | tf_op jit(solution)/shard_map/pallas_call | solution.py:143
  187.7 5.3 %all-to-all-start.2 = ((bf16[4,512,256]{2,1,0:T(8,128)(2,1)}), bf16[4,512,256]{2,1,0:T(8,128)(2,1)S(1)}, u32[]{:S(2)}, u32[]{:S(2)}) async-start(bf16[4,512,256]{2,1,0:T(8,128)(2,1)} %get-tuple-element.73), calls=%async_computation.2 | async-start | bytes 2097152 | tf_op jit(solution)/shard_map/all_to_all | solution.py:479
  193.0 8.3 %shard_map.139 = (f32[8192,128]{1,0:T(8,128)}, f32[3,8,128]{2,1,0:T(8,128)}) custom-call(f32[2,8,128]{2,1,0:T(8,128)} %add_add_fusion.4.sums, f32[3,8,128]{2,1,0:T(8,128)} %get-tuple-element.143.params, f32[1024]{0:T(1024)} %fusion.22.keep, f32[8192,128]{1,0:T(8,128)} %get-tuple-element.72.pre, f32[8192,128]{1,0:T(8,128)} %get-tuple-element.75.states.before, ...), custom_call_target="tpu_custom_call" | custom-call | flops 25165824 | bytes 16777216 | tf_op jit(solution)/shard_map/pallas_call | solution.py:245
  216.5 7.5 %shard_map.140 = (bf16[1024,1024]{1,0:T(8,128)(2,1)}, bf16[4,1024,256]{2,1,0:T(8,128)(2,1)}) custom-call(f32[2,8,128]{2,1,0:T(8,128)} %add_add_fusion.4.sums, f32[3,8,128]{2,1,0:T(8,128)} %get-tuple-element.143.params, f32[3,8,128]{2,1,0:T(8,128)} %add_add_fusion.2.totals, f32[8192,128]{1,0:T(8,128)} %get-tuple-element.83.carried, ...), custom_call_target="tpu_custom_call" | custom-call | flops 2147483648 | bytes 16777216 | tf_op jit(solution)/shard_map/pallas_call | solution.py:305
  224.0 8.5 %shard_map.141 = bf16[4,4,2,256,256]{4,3,2,1,0:T(8,128)(2,1)} custom-call(bf16[4,1024,256]{2,1,0:T(8,128)(2,1)} %get-tuple-element.69.xs, bf16[4,1024,256]{2,1,0:T(8,128)(2,1)} %collective-permute-done.19.xo, bf16[1024,1024]{1,0:T(8,128)(2,1)} %get-tuple-element.85.dpre), custom_call_target="tpu_custom_call" | custom-call | flops 4294967296 | bytes 10485760 | tf_op jit(solution)/shard_map/pallas_call | solution.py:383
  232.6 5.8 %all-to-all-start.4 = ((bf16[4,512,256]{2,1,0:T(8,128)(2,1)}), bf16[4,512,256]{2,1,0:T(8,128)(2,1)S(1)}, u32[]{:S(2)}, u32[]{:S(2)}) async-start(bf16[4,512,256]{2,1,0:T(8,128)(2,1)} %get-tuple-element.80), calls=%async_computation.4 | async-start | bytes 2097152 | tf_op jit(solution)/shard_map/all_to_all | solution.py:479
  238.3 5.5 %shard_map.142.rest_0_ = bf16[4,1024,256]{2,1,0:T(8,128)(2,1)} custom-call(bf16[1024,1024]{1,0:T(8,128)(2,1)} %get-tuple-element.85.dpre, bf16[4,4,2,256,256]{4,3,2,1,0:T(8,128)(2,1)} %bitcast.79), custom_call_target="tpu_custom_call" | custom-call | flops 2147483648 | bytes 6291456 | tf_op jit(solution)/shard_map/pallas_call | solution.py:332
  245.2 9.0 %shard_map.143 = (f32[8192,128]{1,0:T(8,128)}, f32[3,8,128]{2,1,0:T(8,128)}) custom-call(f32[2,8,128]{2,1,0:T(8,128)} %fusion.12.sums, f32[3,8,128]{2,1,0:T(8,128)} %get-tuple-element.144.params, f32[1024]{0:T(1024)} %fusion.22.keep, f32[8192,128]{1,0:T(8,128)} %get-tuple-element.68.pre, f32[8192,128]{1,0:T(8,128)} %get-tuple-element.81.states.before, ...), custom_call_target="tpu_custom_call" | custom-call | flops 25165824 | bytes 16777216 | tf_op jit(solution)/shard_map/pallas_call | solution.py:245
  269.2 7.7 %shard_map.144 = (bf16[1024,1024]{1,0:T(8,128)(2,1)}, bf16[4,1024,256]{2,1,0:T(8,128)(2,1)}) custom-call(f32[2,8,128]{2,1,0:T(8,128)} %fusion.12.sums, f32[3,8,128]{2,1,0:T(8,128)} %get-tuple-element.144.params, f32[3,8,128]{2,1,0:T(8,128)} %add_add_fusion.totals, f32[8192,128]{1,0:T(8,128)} %get-tuple-element.89.carried, ...), custom_call_target="tpu_custom_call" | custom-call | flops 2147483648 | bytes 16777216 | tf_op jit(solution)/shard_map/pallas_call | solution.py:305
  277.0 5.6 %shard_map.148.same = bf16[4,1024,256]{2,1,0:T(8,128)(2,1)} custom-call(bf16[1024,1024]{1,0:T(8,128)(2,1)} %get-tuple-element.90.dpre, bf16[4,4,2,256,256]{4,3,2,1,0:T(8,128)(2,1)} %bitcast_dynamic-update-slice_fusion.w), custom_call_target="tpu_custom_call" | custom-call | flops 2147483648 | bytes 6291456 | tf_op jit(solution)/shard_map/pallas_call | solution.py:332
  291.4 5.1 %all-to-all-start.5 = ((bf16[4,1536,256]{2,1,0:T(8,128)(2,1)}), bf16[4,1536,256]{2,1,0:T(8,128)(2,1)S(1)}, u32[]{:S(2)}, u32[]{:S(2)}) async-start(bf16[4,1536,256]{2,1,0:T(8,128)(2,1)} %shard_map.149), calls=%async_computation.6 | async-start | bytes 6291456 | tf_op jit(solution)/shard_map/all_to_all | solution.py:479
  296.5 8.4 %shard_map.145 = bf16[4,4,2,256,256]{4,3,2,1,0:T(8,128)(2,1)} custom-call(bf16[4,1024,256]{2,1,0:T(8,128)(2,1)} %all-to-all-done.xs, bf16[4,1024,256]{2,1,0:T(8,128)(2,1)} %collective-permute-done.11.xo, bf16[1024,1024]{1,0:T(8,128)(2,1)} %get-tuple-element.90.dpre), custom_call_target="tpu_custom_call" | custom-call | flops 4294967296 | bytes 10485760 | tf_op jit(solution)/shard_map/pallas_call | solution.py:383
  321.4 14.2 %collective-permute-done.39 = bf16[4,2,256,256]{3,2,1,0:T(8,128)(2,1)} collective-permute-done((bf16[4,2,256,256]{3,2,1,0:T(8,128)(2,1)}, bf16[4,2,256,256]{3,2,1,0:T(8,128)(2,1)}, u32[]{:S(2)}, u32[]{:S(2)}) %collective-permute-start.39) | collective-permute-done | bytes 1048608 | tf_op jit(solution)/shard_map/ppermute | solution.py:444
  335.6 21.1 %collective-permute-done.40 = bf16[4,2,256,256]{3,2,1,0:T(8,128)(2,1)} collective-permute-done((bf16[4,2,256,256]{3,2,1,0:T(8,128)(2,1)}, bf16[4,2,256,256]{3,2,1,0:T(8,128)(2,1)}, u32[]{:S(2)}, u32[]{:S(2)}) %collective-permute-start.40) | collective-permute-done | bytes 1048608 | tf_op jit(solution)/shard_map/ppermute | solution.py:444
  364.8 6.6 %all-to-all-start.6 = ((bf16[4,256,512]{2,1,0:T(8,128)(2,1)}), bf16[4,256,512]{2,1,0:T(8,128)(2,1)}, u32[]{:S(2)}, u32[]{:S(2)}) async-start(bf16[4,256,512]{2,1,0:T(8,128)(2,1)} %pad_maximum_fusion.4), calls=%async_computation.7 | async-start | bytes 2097152 | tf_op jit(solution)/shard_map/all_to_all | solution.py:479
  379.5 14.8 %all-to-all-done.6 = bf16[4,256,512]{2,1,0:T(8,128)(2,1)} async-done(((bf16[4,256,512]{2,1,0:T(8,128)(2,1)}), bf16[4,256,512]{2,1,0:T(8,128)(2,1)}, u32[]{:S(2)}, u32[]{:S(2)}) %all-to-all-start.6) | async-done | bytes 1048608 | tf_op jit(solution)/shard_map/all_to_all | solution.py:479
  (236 shorter events, 150.9 us)
Async XLA Ops:
  9.6 8.9 %collective-permute-start = (bf16[2,1024,256]{2,1,0:T(8,128)(2,1)}, bf16[2,1024,256]{2,1,0:T(8,128)(2,1)S(1)}, u32[]{:S(2)}, u32[]{:S(2)}) collective-permute-start(bf16[2,1024,256]{2,1,0:T(8,128)(2,1)} %constant_dynamic-slice_fusion.7), channel_id=1, source_target_pairs={{0,1},{1,0},{2,3},{3,2},{4,5},{5,4},{6,7},{7,6},{8,9},{9,8},{10,11... | collective-permute-start | bytes 3145736 | tf_op jit(solution)/shard_map/ppermute | solution.py:444
  11.9 13.2 %collective-permute-start.1 = (bf16[256,512]{1,0:T(8,128)(2,1)S(1)}, bf16[256,512]{1,0:T(8,128)(2,1)}, u32[]{:S(2)}, u32[]{:S(2)}) collective-permute-start(bf16[256,512]{1,0:T(8,128)(2,1)S(1)} %get-tuple-element.57), channel_id=1, source_target_pairs={{0,8},{1,9},{2,10},{3,11},{4,12},{5,13},{6,14},{7,15},{8,0},{9,1},... | collective-permute-start | bytes 786440 | tf_op jit(solution)/shard_map/ppermute | solution.py:444
  12.3 21.4 %collective-permute-start.2 = (bf16[256,512]{1,0:T(8,128)(2,1)S(1)}, bf16[256,512]{1,0:T(8,128)(2,1)}, u32[]{:S(2)}, u32[]{:S(2)}) collective-permute-start(bf16[256,512]{1,0:T(8,128)(2,1)S(1)} %get-tuple-element.57), channel_id=1, source_target_pairs={{0,16},{1,17},{2,18},{3,19},{4,20},{5,21},{6,22},{7,23},{8,24},{9,... | collective-permute-start | bytes 786440 | tf_op jit(solution)/shard_map/ppermute | solution.py:444
  13.0 20.7 %collective-permute-start.3 = (bf16[256,512]{1,0:T(8,128)(2,1)S(1)}, bf16[256,512]{1,0:T(8,128)(2,1)}, u32[]{:S(2)}, u32[]{:S(2)}) collective-permute-start(bf16[256,512]{1,0:T(8,128)(2,1)S(1)} %get-tuple-element.57), channel_id=1, source_target_pairs={{0,24},{1,25},{2,26},{3,27},{4,28},{5,29},{6,30},{7,31},{8,16},{9,... | collective-permute-start | bytes 786440 | tf_op jit(solution)/shard_map/ppermute | solution.py:444
  33.8 75.7 %all-to-all-start = ((bf16[4,1024,256]{2,1,0:T(8,128)(2,1)}), bf16[4,1024,256]{2,1,0:T(8,128)(2,1)}, u32[]{:S(2)}, u32[]{:S(2)}) async-start(bf16[4,1024,256]{2,1,0:T(8,128)(2,1)} %pad_maximum_fusion), calls=%async_computation | async-start | bytes 4194304 | tf_op jit(solution)/shard_map/all_to_all | solution.py:479
  42.9 59.8 %all-gather.5.cloned.1.call-start = ((), (), s32[]{:S(2)}) async-start(), calls=%async_computation.9 | async-start | bytes 1310720 | tf_op jit(solution)/shard_map/all_gather | solution.py:494
  46.8 111.5 %all-gather.7.cloned.1.call-start = ((), (), s32[]{:S(2)}) async-start(), calls=%async_computation.10 | async-start | bytes 5242880 | tf_op jit(solution)/shard_map/all_gather | solution.py:494
  47.9 54.8 %collective-permute-start.7 = (bf16[4,2,256,256]{3,2,1,0:T(8,128)(2,1)S(1)}, bf16[4,2,256,256]{3,2,1,0:T(8,128)(2,1)}, u32[]{:S(2)}, u32[]{:S(2)}) collective-permute-start(bf16[4,2,256,256]{3,2,1,0:T(8,128)(2,1)S(1)} %fusion.6), channel_id=1, source_target_pairs={{0,2},{1,3},{2,0},{3,1},{4,6},{5,7},{6,4},{7,5},{8,10},{9,11},{10,... | collective-permute-start | bytes 3145736 | tf_op jit(solution)/shard_map/ppermute | solution.py:444
  49.4 55.5 %collective-permute-start.8 = (bf16[4,2,256,256]{3,2,1,0:T(8,128)(2,1)S(1)}, bf16[4,2,256,256]{3,2,1,0:T(8,128)(2,1)}, u32[]{:S(2)}, u32[]{:S(2)}) collective-permute-start(bf16[4,2,256,256]{3,2,1,0:T(8,128)(2,1)S(1)} %fusion.6), channel_id=1, source_target_pairs={{0,4},{1,5},{2,6},{3,7},{4,0},{5,1},{6,2},{7,3},{8,12},{9,13},{10,... | collective-permute-start | bytes 3145736 | tf_op jit(solution)/shard_map/ppermute | solution.py:444
  50.0 57.2 %collective-permute-start.9 = (bf16[4,2,256,256]{3,2,1,0:T(8,128)(2,1)S(1)}, bf16[4,2,256,256]{3,2,1,0:T(8,128)(2,1)}, u32[]{:S(2)}, u32[]{:S(2)}) collective-permute-start(bf16[4,2,256,256]{3,2,1,0:T(8,128)(2,1)S(1)} %fusion.6), channel_id=1, source_target_pairs={{0,6},{1,7},{2,4},{3,5},{4,2},{5,3},{6,0},{7,1},{8,14},{9,15},{10,... | collective-permute-start | bytes 3145736 | tf_op jit(solution)/shard_map/ppermute | solution.py:444
  109.5 31.1 %all-to-all-start.1 = ((bf16[4,512,256]{2,1,0:T(8,128)(2,1)}), bf16[4,512,256]{2,1,0:T(8,128)(2,1)S(1)}, u32[]{:S(2)}, u32[]{:S(2)}) async-start(bf16[4,512,256]{2,1,0:T(8,128)(2,1)} %pad_maximum_fusion.2), calls=%async_computation.1 | async-start | bytes 2097152 | tf_op jit(solution)/shard_map/all_to_all | solution.py:479
  131.7 8.3 %collective-permute-start.16 = (f32[28,128]{1,0:T(8,128)S(1)}, f32[28,128]{1,0:T(8,128)S(1)}, u32[]{:S(2)}, u32[]{:S(2)}) collective-permute-start(f32[28,128]{1,0:T(8,128)S(1)} %pad_maximum_fusion.11), channel_id=1, source_target_pairs={{0,16},{1,17},{2,18},{3,19},{4,20},{5,21},{6,22},{7,23},{8,24},{9,... | collective-permute-start | bytes 43016 | tf_op jit(solution)/shard_map/ppermute | solution.py:444
  133.6 6.4 %collective-permute-start.15 = (f32[28,128]{1,0:T(8,128)S(1)}, f32[28,128]{1,0:T(8,128)S(1)}, u32[]{:S(2)}, u32[]{:S(2)}) collective-permute-start(f32[28,128]{1,0:T(8,128)S(1)} %pad_maximum_fusion.11), channel_id=1, source_target_pairs={{0,8},{1,9},{2,10},{3,11},{4,12},{5,13},{6,14},{7,15},{8,0},{9,1},... | collective-permute-start | bytes 43016 | tf_op jit(solution)/shard_map/ppermute | solution.py:444
  147.7 40.0 %all-to-all-start.3 = ((bf16[4,512,256]{2,1,0:T(8,128)(2,1)}), bf16[4,512,256]{2,1,0:T(8,128)(2,1)S(1)}, u32[]{:S(2)}, u32[]{:S(2)}) async-start(bf16[4,512,256]{2,1,0:T(8,128)(2,1)} %pad_maximum_fusion.3), calls=%async_computation.3 | async-start | bytes 2097152 | tf_op jit(solution)/shard_map/all_to_all | solution.py:479
  187.7 28.8 %all-to-all-start.2 = ((bf16[4,512,256]{2,1,0:T(8,128)(2,1)}), bf16[4,512,256]{2,1,0:T(8,128)(2,1)S(1)}, u32[]{:S(2)}, u32[]{:S(2)}) async-start(bf16[4,512,256]{2,1,0:T(8,128)(2,1)} %get-tuple-element.73), calls=%async_computation.2 | async-start | bytes 2097152 | tf_op jit(solution)/shard_map/all_to_all | solution.py:479
  193.0 93.7 %reduce-scatter.2.cloned.1.call-start = ((), (), s32[]{:S(2)}) async-start(), calls=%async_computation.8 | async-start | bytes 5242880 | tf_op jit(solution)/shard_map/reduce_scatter | solution.py:501
  208.9 6.9 %collective-permute-start.30 = (f32[3,8,128]{2,1,0:T(8,128)S(1)}, f32[3,8,128]{2,1,0:T(8,128)S(1)}, u32[]{:S(2)}, u32[]{:S(2)}) collective-permute-start(f32[3,8,128]{2,1,0:T(8,128)S(1)} %add_add_fusion.3), channel_id=1, source_target_pairs={{0,16},{1,17},{2,18},{3,19},{4,20},{5,21},{6,22},{7,23},{8,24},{9,... | collective-permute-start | bytes 36872 | tf_op jit(solution)/shard_map/ppermute | solution.py:444
  232.5 11.3 %collective-permute-start.32 = (bf16[4,1024,256]{2,1,0:T(8,128)(2,1)}, bf16[4,1024,256]{2,1,0:T(8,128)(2,1)S(1)}, u32[]{:S(2)}, u32[]{:S(2)}) collective-permute-start(bf16[4,1024,256]{2,1,0:T(8,128)(2,1)} %get-tuple-element.86), channel_id=1, source_target_pairs={{0,1},{1,0},{2,3},{3,2},{4,5},{5,4},{6,7},{7,6},{8,9},{9,8},{10,11... | collective-permute-start | bytes 6291464 | tf_op jit(solution)/shard_map/ppermute | solution.py:444
  232.6 36.6 %all-to-all-start.4 = ((bf16[4,512,256]{2,1,0:T(8,128)(2,1)}), bf16[4,512,256]{2,1,0:T(8,128)(2,1)S(1)}, u32[]{:S(2)}, u32[]{:S(2)}) async-start(bf16[4,512,256]{2,1,0:T(8,128)(2,1)} %get-tuple-element.80), calls=%async_computation.4 | async-start | bytes 2097152 | tf_op jit(solution)/shard_map/all_to_all | solution.py:479
  291.4 73.4 %all-to-all-start.5 = ((bf16[4,1536,256]{2,1,0:T(8,128)(2,1)}), bf16[4,1536,256]{2,1,0:T(8,128)(2,1)S(1)}, u32[]{:S(2)}, u32[]{:S(2)}) async-start(bf16[4,1536,256]{2,1,0:T(8,128)(2,1)} %shard_map.149), calls=%async_computation.6 | async-start | bytes 6291456 | tf_op jit(solution)/shard_map/all_to_all | solution.py:479
  309.2 26.4 %collective-permute-start.39 = (bf16[4,2,256,256]{3,2,1,0:T(8,128)(2,1)}, bf16[4,2,256,256]{3,2,1,0:T(8,128)(2,1)}, u32[]{:S(2)}, u32[]{:S(2)}) collective-permute-start(bf16[4,2,256,256]{3,2,1,0:T(8,128)(2,1)} %get-tuple-element.123), channel_id=1, source_target_pairs={{0,2},{1,3},{2,0},{3,1},{4,6},{5,7},{6,4},{7,5},{8,10},{9,11},{10,... | collective-permute-start | bytes 3145736 | tf_op jit(solution)/shard_map/ppermute | solution.py:444
  309.8 46.8 %collective-permute-start.40 = (bf16[4,2,256,256]{3,2,1,0:T(8,128)(2,1)}, bf16[4,2,256,256]{3,2,1,0:T(8,128)(2,1)}, u32[]{:S(2)}, u32[]{:S(2)}) collective-permute-start(bf16[4,2,256,256]{3,2,1,0:T(8,128)(2,1)} %get-tuple-element.122), channel_id=1, source_target_pairs={{0,4},{1,5},{2,6},{3,7},{4,0},{5,1},{6,2},{7,3},{8,12},{9,13},{10,... | collective-permute-start | bytes 3145736 | tf_op jit(solution)/shard_map/ppermute | solution.py:444
  311.2 45.5 %collective-permute-start.41 = (bf16[4,2,256,256]{3,2,1,0:T(8,128)(2,1)}, bf16[4,2,256,256]{3,2,1,0:T(8,128)(2,1)}, u32[]{:S(2)}, u32[]{:S(2)}) collective-permute-start(bf16[4,2,256,256]{3,2,1,0:T(8,128)(2,1)} %get-tuple-element.121), channel_id=1, source_target_pairs={{0,6},{1,7},{2,4},{3,5},{4,2},{5,3},{6,0},{7,1},{8,14},{9,15},{10,... | collective-permute-start | bytes 3145736 | tf_op jit(solution)/shard_map/ppermute | solution.py:444
  364.8 29.6 %all-to-all-start.6 = ((bf16[4,256,512]{2,1,0:T(8,128)(2,1)}), bf16[4,256,512]{2,1,0:T(8,128)(2,1)}, u32[]{:S(2)}, u32[]{:S(2)}) async-start(bf16[4,256,512]{2,1,0:T(8,128)(2,1)} %pad_maximum_fusion.4), calls=%async_computation.7 | async-start | bytes 2097152 | tf_op jit(solution)/shard_map/all_to_all | solution.py:479
  (58 other events, 313.3 us)
Sparse Core Ops, SparseCore 0:
  46.9 55.6 all-gather.4
  104.5 53.7 all-gather.6
  232.6 54.0 reduce-scatter.1

commit v3 on v2

--- a/solution.py
+++ b/solution.py
@@ -510,7 +510,9 @@
     shards = [weights[0]] + [over_wide(weights[0], m) for m in range(1, wide)]
     x = by_half(frames, 0, LENGTH)
     cut = LENGTH // 2
-    x, shards, keep, grad_out, second = lax.optimization_barrier((x, shards, keep, grad_out, second))
+    x, shards[2], keep = lax.optimization_barrier((x, shards[2], keep))
+    shards[3], second = lax.optimization_barrier((shards[3], second))
+    shards, grad_out = lax.optimization_barrier((shards, grad_out))
     mats = [None, gathered_late(second)]
     xs = exchange(x)
     line = jnp.stack(halves(jnp.stack(shards)), 1)

time: 409 us -> 403 us (0.985)
    all_gather x2, waiting for transfers between devices: 49.5 us -> 13.7 us  [gathered_late(): return lax.all_gather(lax.all_gather(both, 'wide'), 'ring')]
    ppermute x49, waiting for transfers between devices: 77.3 us -> 109 us  [send(): return lax.ppermute(x, AXES, pairs)]
  transfers between devices with their start and end apart: 59 -> 59, of which waited for: 36 -> 34; matrix products, arithmetic and copies ran while one was open for 11% -> 11% of each run, Pallas kernels for 21% -> 21%
where the time goes in v3:
time: 403 us; the launch traced here: 398 us
  waiting for transfers between devices  144 us (36%)
  Pallas kernels  104 us (26%)
  starting transfers between devices  84.1 us (21%)
  local copies, waits for them, and re-layouts  28.6 us (7%)
  other arithmetic  22.7 us (6%)
  between operations  14.3 us (4%)
    ppermute x49, waiting for transfers between devices, send(): return lax.ppermute(x, AXES, pairs)  109 us
    ppermute x49, starting transfers between devices, send(): return lax.ppermute(x, AXES, pairs)  43.3 us
    all_to_all x7, starting transfers between devices, exchange(): return lax.all_to_all(x, 'wide', 0, 0, tiled=True)  40.7 us
    pallas_call x2, Pallas kernels, product(): pl.pallas_call(functools.partial(product_kernel, by_row), grid=(rows // s...  18.5 us
    all_to_all x7, waiting for transfers between devices, exchange(): return lax.all_to_all(x, 'wide', 0, 0, tiled=True)  17.3 us
    pallas_call x2, Pallas kernels, backward(): pl.pallas_call(functools.partial(backward_kernel, count, terms), grid=(ro...  17.2 us
    pallas_call x2, Pallas kernels, outer(): pl.pallas_call(functools.partial(outer_kernel, by_row), grid=(blocks,), i...  16.9 us
    pallas_call x2, Pallas kernels, spread(): pl.pallas_call(functools.partial(spread_kernel, count, by_row), grid=(row...  15.2 us
  transfers between devices with their start and end apart: 59, of which 34 were waited for; matrix products, arithmetic and copies ran while one was open for 11% of the time, Pallas kernels for 21%

profile of v3, /device:TPU:28, one launch (start us, length us, event | category | flops | bytes accessed | tf_op | source)
XLA Modules:
  0.0 397.6 jit_solution(11377772119730302410)
XLA Ops:
  23.8 12.3 %collective-permute-done.1 = bf16[256,512]{1,0:T(8,128)(2,1)S(1)} collective-permute-done((bf16[256,512]{1,0:T(8,128)(2,1)}, bf16[256,512]{1,0:T(8,128)(2,1)S(1)}, u32[]{:S(2)}, u32[]{:S(2)}) %collective-permute-start.1) | collective-permute-done | bytes 262176 | tf_op jit(solution)/shard_map/ppermute | solution.py:444
  36.1 5.8 %all-to-all-start = ((bf16[4,1024,256]{2,1,0:T(8,128)(2,1)}), bf16[4,1024,256]{2,1,0:T(8,128)(2,1)}, u32[]{:S(2)}, u32[]{:S(2)}) async-start(bf16[4,1024,256]{2,1,0:T(8,128)(2,1)} %pad_maximum_fusion), calls=%async_computation | async-start | bytes 4194304 | tf_op jit(solution)/shard_map/all_to_all | solution.py:479
  56.9 13.6 %all-gather.5.cloned.1.call-done = bf16[8,256,256]{2,1,0:T(8,128)(2,1)} async-done(((bf16[2,256,256]{2,1,0:T(8,128)(2,1)}), bf16[8,256,256]{2,1,0:T(8,128)(2,1)}) %all-gather.5.cloned.1.call-update) | async-done | bytes 1048592 | tf_op jit(solution)/shard_map/all_gather | solution.py:494
  74.7 20.4 %collective-permute-done.8 = bf16[4,2,256,256]{3,2,1,0:T(8,128)(2,1)} collective-permute-done((bf16[4,2,256,256]{3,2,1,0:T(8,128)(2,1)S(1)}, bf16[4,2,256,256]{3,2,1,0:T(8,128)(2,1)}, u32[]{:S(2)}, u32[]{:S(2)}) %collective-permute-start.8) | collective-permute-done | bytes 1048608 | tf_op jit(solution)/shard_map/ppermute | solution.py:444
  102.8 5.6 %all-to-all-start.1 = ((bf16[4,512,256]{2,1,0:T(8,128)(2,1)}), bf16[4,512,256]{2,1,0:T(8,128)(2,1)S(1)}, u32[]{:S(2)}, u32[]{:S(2)}) async-start(bf16[4,512,256]{2,1,0:T(8,128)(2,1)} %pad_maximum_fusion.2), calls=%async_computation.1 | async-start | bytes 2097152 | tf_op jit(solution)/shard_map/all_to_all | solution.py:479
  108.4 9.3 %shard_map.135 = (f32[8192,128]{1,0:T(8,128)}, f32[2,8,128]{2,1,0:T(8,128)}) custom-call(bf16[4,1024,256]{2,1,0:T(8,128)(2,1)} %all-to-all-done.xs, bf16[4,1024,256]{2,1,0:T(8,128)(2,1)} %collective-permute-done.11.xo, bf16[4,4,2,256,256]{4,3,2,1,0:T(8,128)(2,1)} %bitcast_dynamic-update-slice_fusion.w), custom_call_target="tpu_custom_call" | custom-call | flops 4294967296 | bytes 12582912 | tf_op jit(solution)/shard_map/pallas_call | solution.py:66
  135.6 6.2 %shard_map.136 = (f32[8192,128]{1,0:T(8,128)}, bf16[4,1024,256]{2,1,0:T(8,128)(2,1)}) custom-call(f32[2,8,128]{2,1,0:T(8,128)} %fusion.12.sums, f32[3,8,128]{2,1,0:T(8,128)} %get-tuple-element.148.params, f32[1024]{0:T(1024)} %fusion.22.keep, f32[8192,128]{1,0:T(8,128)} %get-tuple-element.72.pre), custom_call_target="tpu_custom_call" | custom-call | flops 12582912 | bytes 10485760 | tf_op jit(solution)/shard_map/pallas_call | solution.py:143
  141.8 5.9 %all-to-all-start.3 = ((bf16[4,512,256]{2,1,0:T(8,128)(2,1)}), bf16[4,512,256]{2,1,0:T(8,128)(2,1)S(1)}, u32[]{:S(2)}, u32[]{:S(2)}) async-start(bf16[4,512,256]{2,1,0:T(8,128)(2,1)} %pad_maximum_fusion.3), calls=%async_computation.3 | async-start | bytes 2097152 | tf_op jit(solution)/shard_map/all_to_all | solution.py:479
  147.6 9.2 %shard_map.137 = (f32[8192,128]{1,0:T(8,128)}, f32[2,8,128]{2,1,0:T(8,128)}) custom-call(bf16[4,1024,256]{2,1,0:T(8,128)(2,1)} %get-tuple-element.73.xs, bf16[4,1024,256]{2,1,0:T(8,128)(2,1)} %collective-permute-done.19.xo, bf16[4,4,2,256,256]{4,3,2,1,0:T(8,128)(2,1)} %bitcast.77), custom_call_target="tpu_custom_call" | custom-call | flops 4294967296 | bytes 12582912 | tf_op jit(solution)/shard_map/pallas_call | solution.py:66
  173.2 6.5 %shard_map.138 = (f32[8192,128]{1,0:T(8,128)}, bf16[4,512,256]{2,1,0:T(8,128)(2,1)}, bf16[4,512,256]{2,1,0:T(8,128)(2,1)}) custom-call(f32[2,8,128]{2,1,0:T(8,128)} %add_add_fusion.4.sums, f32[3,8,128]{2,1,0:T(8,128)} %get-tuple-element.147.params, f32[1024]{0:T(1024)} %fusion.22.keep, f32[8192,128]{1,0:T(8,128)} %get-tuple-element.76.pre), custom_call_target="tpu_custom_call" | custom-call | flops 12582912 | bytes 10485760 | tf_op jit(solution)/shard_map/pallas_call | solution.py:143
  179.7 5.9 %all-to-all-start.2 = ((bf16[4,512,256]{2,1,0:T(8,128)(2,1)}), bf16[4,512,256]{2,1,0:T(8,128)(2,1)S(1)}, u32[]{:S(2)}, u32[]{:S(2)}) async-start(bf16[4,512,256]{2,1,0:T(8,128)(2,1)} %get-tuple-element.77), calls=%async_computation.2 | async-start | bytes 2097152 | tf_op jit(solution)/shard_map/all_to_all | solution.py:479
  185.6 8.3 %shard_map.139 = (f32[8192,128]{1,0:T(8,128)}, f32[3,8,128]{2,1,0:T(8,128)}) custom-call(f32[2,8,128]{2,1,0:T(8,128)} %add_add_fusion.4.sums, f32[3,8,128]{2,1,0:T(8,128)} %get-tuple-element.147.params, f32[1024]{0:T(1024)} %fusion.22.keep, f32[8192,128]{1,0:T(8,128)} %get-tuple-element.76.pre, f32[8192,128]{1,0:T(8,128)} %get-tuple-element.79.states.before, ...), custom_call_target="tpu_custom_call" | custom-call | flops 25165824 | bytes 16777216 | tf_op jit(solution)/shard_map/pallas_call | solution.py:245
  210.6 7.5 %shard_map.140 = (bf16[1024,1024]{1,0:T(8,128)(2,1)}, bf16[4,1024,256]{2,1,0:T(8,128)(2,1)}) custom-call(f32[2,8,128]{2,1,0:T(8,128)} %add_add_fusion.4.sums, f32[3,8,128]{2,1,0:T(8,128)} %get-tuple-element.147.params, f32[3,8,128]{2,1,0:T(8,128)} %add_add_fusion.2.totals, f32[8192,128]{1,0:T(8,128)} %get-tuple-element.87.carried, ...), custom_call_target="tpu_custom_call" | custom-call | flops 2147483648 | bytes 16777216 | tf_op jit(solution)/shard_map/pallas_call | solution.py:305
  218.0 8.5 %shard_map.141 = bf16[4,4,2,256,256]{4,3,2,1,0:T(8,128)(2,1)} custom-call(bf16[4,1024,256]{2,1,0:T(8,128)(2,1)} %get-tuple-element.73.xs, bf16[4,1024,256]{2,1,0:T(8,128)(2,1)} %collective-permute-done.19.xo, bf16[1024,1024]{1,0:T(8,128)(2,1)} %get-tuple-element.89.dpre), custom_call_target="tpu_custom_call" | custom-call | flops 4294967296 | bytes 10485760 | tf_op jit(solution)/shard_map/pallas_call | solution.py:383
  226.6 5.9 %all-to-all-start.4 = ((bf16[4,512,256]{2,1,0:T(8,128)(2,1)}), bf16[4,512,256]{2,1,0:T(8,128)(2,1)S(1)}, u32[]{:S(2)}, u32[]{:S(2)}) async-start(bf16[4,512,256]{2,1,0:T(8,128)(2,1)} %get-tuple-element.84), calls=%async_computation.4 | async-start | bytes 2097152 | tf_op jit(solution)/shard_map/all_to_all | solution.py:479
  232.5 5.5 %shard_map.142.rest_0_ = bf16[4,1024,256]{2,1,0:T(8,128)(2,1)} custom-call(bf16[1024,1024]{1,0:T(8,128)(2,1)} %get-tuple-element.89.dpre, bf16[4,4,2,256,256]{4,3,2,1,0:T(8,128)(2,1)} %bitcast.79), custom_call_target="tpu_custom_call" | custom-call | flops 2147483648 | bytes 6291456 | tf_op jit(solution)/shard_map/pallas_call | solution.py:332
  239.3 8.9 %shard_map.143 = (f32[8192,128]{1,0:T(8,128)}, f32[3,8,128]{2,1,0:T(8,128)}) custom-call(f32[2,8,128]{2,1,0:T(8,128)} %fusion.12.sums, f32[3,8,128]{2,1,0:T(8,128)} %get-tuple-element.148.params, f32[1024]{0:T(1024)} %fusion.22.keep, f32[8192,128]{1,0:T(8,128)} %get-tuple-element.72.pre, f32[8192,128]{1,0:T(8,128)} %get-tuple-element.85.states.before, ...), custom_call_target="tpu_custom_call" | custom-call | flops 25165824 | bytes 16777216 | tf_op jit(solution)/shard_map/pallas_call | solution.py:245
  263.6 7.7 %shard_map.144 = (bf16[1024,1024]{1,0:T(8,128)(2,1)}, bf16[4,1024,256]{2,1,0:T(8,128)(2,1)}) custom-call(f32[2,8,128]{2,1,0:T(8,128)} %fusion.12.sums, f32[3,8,128]{2,1,0:T(8,128)} %get-tuple-element.148.params, f32[3,8,128]{2,1,0:T(8,128)} %add_add_fusion.totals, f32[8192,128]{1,0:T(8,128)} %get-tuple-element.93.carried, ...), custom_call_target="tpu_custom_call" | custom-call | flops 2147483648 | bytes 16777216 | tf_op jit(solution)/shard_map/pallas_call | solution.py:305
  271.4 5.6 %shard_map.148.same = bf16[4,1024,256]{2,1,0:T(8,128)(2,1)} custom-call(bf16[1024,1024]{1,0:T(8,128)(2,1)} %get-tuple-element.94.dpre, bf16[4,4,2,256,256]{4,3,2,1,0:T(8,128)(2,1)} %bitcast_dynamic-update-slice_fusion.w), custom_call_target="tpu_custom_call" | custom-call | flops 2147483648 | bytes 6291456 | tf_op jit(solution)/shard_map/pallas_call | solution.py:332
  290.7 8.4 %shard_map.145 = bf16[4,4,2,256,256]{4,3,2,1,0:T(8,128)(2,1)} custom-call(bf16[4,1024,256]{2,1,0:T(8,128)(2,1)} %all-to-all-done.xs, bf16[4,1024,256]{2,1,0:T(8,128)(2,1)} %collective-permute-done.11.xo, bf16[1024,1024]{1,0:T(8,128)(2,1)} %get-tuple-element.94.dpre), custom_call_target="tpu_custom_call" | custom-call | flops 4294967296 | bytes 10485760 | tf_op jit(solution)/shard_map/pallas_call | solution.py:383
  315.6 14.2 %collective-permute-done.39 = bf16[4,2,256,256]{3,2,1,0:T(8,128)(2,1)} collective-permute-done((bf16[4,2,256,256]{3,2,1,0:T(8,128)(2,1)}, bf16[4,2,256,256]{3,2,1,0:T(8,128)(2,1)}, u32[]{:S(2)}, u32[]{:S(2)}) %collective-permute-start.39) | collective-permute-done | bytes 1048608 | tf_op jit(solution)/shard_map/ppermute | solution.py:444
  329.8 21.1 %collective-permute-done.40 = bf16[4,2,256,256]{3,2,1,0:T(8,128)(2,1)} collective-permute-done((bf16[4,2,256,256]{3,2,1,0:T(8,128)(2,1)}, bf16[4,2,256,256]{3,2,1,0:T(8,128)(2,1)}, u32[]{:S(2)}, u32[]{:S(2)}) %collective-permute-start.40) | collective-permute-done | bytes 1048608 | tf_op jit(solution)/shard_map/ppermute | solution.py:444
  359.0 6.6 %all-to-all-start.6 = ((bf16[4,256,512]{2,1,0:T(8,128)(2,1)}), bf16[4,256,512]{2,1,0:T(8,128)(2,1)}, u32[]{:S(2)}, u32[]{:S(2)}) async-start(bf16[4,256,512]{2,1,0:T(8,128)(2,1)} %pad_maximum_fusion.4), calls=%async_computation.7 | async-start | bytes 2097152 | tf_op jit(solution)/shard_map/all_to_all | solution.py:479
  373.8 14.8 %all-to-all-done.6 = bf16[4,256,512]{2,1,0:T(8,128)(2,1)} async-done(((bf16[4,256,512]{2,1,0:T(8,128)(2,1)}), bf16[4,256,512]{2,1,0:T(8,128)(2,1)}, u32[]{:S(2)}, u32[]{:S(2)}) %all-to-all-start.6) | async-done | bytes 1048608 | tf_op jit(solution)/shard_map/all_to_all | solution.py:479
  (240 shorter events, 159.5 us)
Async XLA Ops:
  7.2 63.4 %all-gather.5.cloned.1.call-start = ((), (), s32[]{:S(2)}) async-start(), calls=%async_computation.9 | async-start | bytes 1310720 | tf_op jit(solution)/shard_map/all_gather | solution.py:494
  9.7 12.1 %collective-permute-start = (bf16[2,1024,256]{2,1,0:T(8,128)(2,1)}, bf16[2,1024,256]{2,1,0:T(8,128)(2,1)S(1)}, u32[]{:S(2)}, u32[]{:S(2)}) collective-permute-start(bf16[2,1024,256]{2,1,0:T(8,128)(2,1)} %constant_dynamic-slice_fusion.7), channel_id=1, source_target_pairs={{0,1},{1,0},{2,3},{3,2},{4,5},{5,4},{6,7},{7,6},{8,9},{9,8},{10,11... | collective-permute-start | bytes 3145736 | tf_op jit(solution)/shard_map/ppermute | solution.py:444
  10.4 11.4 %collective-permute-start.4 = (bf16[256,512]{1,0:T(8,128)(2,1)}, bf16[256,512]{1,0:T(8,128)(2,1)}, u32[]{:S(2)}, u32[]{:S(2)}) collective-permute-start(bf16[256,512]{1,0:T(8,128)(2,1)} %get-tuple-element.61), channel_id=1, source_target_pairs={{0,24},{1,25},{2,26},{3,27},{4,28},{5,29},{6,30},{7,31},{8,16},{9,... | collective-permute-start | bytes 786440 | tf_op jit(solution)/shard_map/ppermute | solution.py:444
  11.8 24.3 %collective-permute-start.1 = (bf16[256,512]{1,0:T(8,128)(2,1)}, bf16[256,512]{1,0:T(8,128)(2,1)S(1)}, u32[]{:S(2)}, u32[]{:S(2)}) collective-permute-start(bf16[256,512]{1,0:T(8,128)(2,1)} %get-tuple-element.61), channel_id=1, source_target_pairs={{0,16},{1,17},{2,18},{3,19},{4,20},{5,21},{6,22},{7,23},{8,24},{9,... | collective-permute-start | bytes 786440 | tf_op jit(solution)/shard_map/ppermute | solution.py:444
  13.5 28.4 %collective-permute-start.3 = (bf16[256,512]{1,0:T(8,128)(2,1)}, bf16[256,512]{1,0:T(8,128)(2,1)}, u32[]{:S(2)}, u32[]{:S(2)}) collective-permute-start(bf16[256,512]{1,0:T(8,128)(2,1)} %get-tuple-element.61), channel_id=1, source_target_pairs={{0,8},{1,9},{2,10},{3,11},{4,12},{5,13},{6,14},{7,15},{8,0},{9,1},... | collective-permute-start | bytes 786440 | tf_op jit(solution)/shard_map/ppermute | solution.py:444
  36.1 66.7 %all-to-all-start = ((bf16[4,1024,256]{2,1,0:T(8,128)(2,1)}), bf16[4,1024,256]{2,1,0:T(8,128)(2,1)}, u32[]{:S(2)}, u32[]{:S(2)}) async-start(bf16[4,1024,256]{2,1,0:T(8,128)(2,1)} %pad_maximum_fusion), calls=%async_computation | async-start | bytes 4194304 | tf_op jit(solution)/shard_map/all_to_all | solution.py:479
  41.9 105.8 %all-gather.7.cloned.1.call-start = ((), (), s32[]{:S(2)}) async-start(), calls=%async_computation.10 | async-start | bytes 5242880 | tf_op jit(solution)/shard_map/all_gather | solution.py:494
  46.3 26.2 %collective-permute-start.7 = (bf16[4,2,256,256]{3,2,1,0:T(8,128)(2,1)S(1)}, bf16[4,2,256,256]{3,2,1,0:T(8,128)(2,1)}, u32[]{:S(2)}, u32[]{:S(2)}) collective-permute-start(bf16[4,2,256,256]{3,2,1,0:T(8,128)(2,1)S(1)} %fusion.6), channel_id=1, source_target_pairs={{0,2},{1,3},{2,0},{3,1},{4,6},{5,7},{6,4},{7,5},{8,10},{9,11},{10,... | collective-permute-start | bytes 3145736 | tf_op jit(solution)/shard_map/ppermute | solution.py:444
  47.8 47.3 %collective-permute-start.8 = (bf16[4,2,256,256]{3,2,1,0:T(8,128)(2,1)S(1)}, bf16[4,2,256,256]{3,2,1,0:T(8,128)(2,1)}, u32[]{:S(2)}, u32[]{:S(2)}) collective-permute-start(bf16[4,2,256,256]{3,2,1,0:T(8,128)(2,1)S(1)} %fusion.6), channel_id=1, source_target_pairs={{0,4},{1,5},{2,6},{3,7},{4,0},{5,1},{6,2},{7,3},{8,12},{9,13},{10,... | collective-permute-start | bytes 3145736 | tf_op jit(solution)/shard_map/ppermute | solution.py:444
  48.3 52.2 %collective-permute-start.9 = (bf16[4,2,256,256]{3,2,1,0:T(8,128)(2,1)S(1)}, bf16[4,2,256,256]{3,2,1,0:T(8,128)(2,1)}, u32[]{:S(2)}, u32[]{:S(2)}) collective-permute-start(bf16[4,2,256,256]{3,2,1,0:T(8,128)(2,1)S(1)} %fusion.6), channel_id=1, source_target_pairs={{0,6},{1,7},{2,4},{3,5},{4,2},{5,3},{6,0},{7,1},{8,14},{9,15},{10,... | collective-permute-start | bytes 3145736 | tf_op jit(solution)/shard_map/ppermute | solution.py:444
  102.8 31.9 %all-to-all-start.1 = ((bf16[4,512,256]{2,1,0:T(8,128)(2,1)}), bf16[4,512,256]{2,1,0:T(8,128)(2,1)S(1)}, u32[]{:S(2)}, u32[]{:S(2)}) async-start(bf16[4,512,256]{2,1,0:T(8,128)(2,1)} %pad_maximum_fusion.2), calls=%async_computation.1 | async-start | bytes 2097152 | tf_op jit(solution)/shard_map/all_to_all | solution.py:479
  126.2 7.8 %collective-permute-start.16 = (f32[28,128]{1,0:T(8,128)S(1)}, f32[28,128]{1,0:T(8,128)S(1)}, u32[]{:S(2)}, u32[]{:S(2)}) collective-permute-start(f32[28,128]{1,0:T(8,128)S(1)} %pad_maximum_fusion.11), channel_id=1, source_target_pairs={{0,16},{1,17},{2,18},{3,19},{4,20},{5,21},{6,22},{7,23},{8,24},{9,... | collective-permute-start | bytes 43016 | tf_op jit(solution)/shard_map/ppermute | solution.py:444
  141.8 37.9 %all-to-all-start.3 = ((bf16[4,512,256]{2,1,0:T(8,128)(2,1)}), bf16[4,512,256]{2,1,0:T(8,128)(2,1)S(1)}, u32[]{:S(2)}, u32[]{:S(2)}) async-start(bf16[4,512,256]{2,1,0:T(8,128)(2,1)} %pad_maximum_fusion.3), calls=%async_computation.3 | async-start | bytes 2097152 | tf_op jit(solution)/shard_map/all_to_all | solution.py:479
  164.4 8.1 %collective-permute-start.24 = (f32[2,8,128]{2,1,0:T(8,128)S(1)}, f32[2,8,128]{2,1,0:T(8,128)S(1)}, u32[]{:S(2)}, u32[]{:S(2)}) collective-permute-start(f32[2,8,128]{2,1,0:T(8,128)S(1)} %add_add_fusion.5), channel_id=1, source_target_pairs={{0,16},{1,17},{2,18},{3,19},{4,20},{5,21},{6,22},{7,23},{8,24},{9,... | collective-permute-start | bytes 24584 | tf_op jit(solution)/shard_map/ppermute | solution.py:444
  179.7 30.9 %all-to-all-start.2 = ((bf16[4,512,256]{2,1,0:T(8,128)(2,1)}), bf16[4,512,256]{2,1,0:T(8,128)(2,1)S(1)}, u32[]{:S(2)}, u32[]{:S(2)}) async-start(bf16[4,512,256]{2,1,0:T(8,128)(2,1)} %get-tuple-element.77), calls=%async_computation.2 | async-start | bytes 2097152 | tf_op jit(solution)/shard_map/all_to_all | solution.py:479
  185.6 95.3 %reduce-scatter.2.cloned.1.call-start = ((), (), s32[]{:S(2)}) async-start(), calls=%async_computation.8 | async-start | bytes 5242880 | tf_op jit(solution)/shard_map/reduce_scatter | solution.py:501
  201.6 8.4 %collective-permute-start.30 = (f32[3,8,128]{2,1,0:T(8,128)S(1)}, f32[3,8,128]{2,1,0:T(8,128)S(1)}, u32[]{:S(2)}, u32[]{:S(2)}) collective-permute-start(f32[3,8,128]{2,1,0:T(8,128)S(1)} %add_add_fusion.3), channel_id=1, source_target_pairs={{0,16},{1,17},{2,18},{3,19},{4,20},{5,21},{6,22},{7,23},{8,24},{9,... | collective-permute-start | bytes 36872 | tf_op jit(solution)/shard_map/ppermute | solution.py:444
  226.5 11.5 %collective-permute-start.32 = (bf16[4,1024,256]{2,1,0:T(8,128)(2,1)}, bf16[4,1024,256]{2,1,0:T(8,128)(2,1)S(1)}, u32[]{:S(2)}, u32[]{:S(2)}) collective-permute-start(bf16[4,1024,256]{2,1,0:T(8,128)(2,1)} %get-tuple-element.90), channel_id=1, source_target_pairs={{0,1},{1,0},{2,3},{3,2},{4,5},{5,4},{6,7},{7,6},{8,9},{9,8},{10,11... | collective-permute-start | bytes 6291464 | tf_op jit(solution)/shard_map/ppermute | solution.py:444
  226.6 36.9 %all-to-all-start.4 = ((bf16[4,512,256]{2,1,0:T(8,128)(2,1)}), bf16[4,512,256]{2,1,0:T(8,128)(2,1)S(1)}, u32[]{:S(2)}, u32[]{:S(2)}) async-start(bf16[4,512,256]{2,1,0:T(8,128)(2,1)} %get-tuple-element.84), calls=%async_computation.4 | async-start | bytes 2097152 | tf_op jit(solution)/shard_map/all_to_all | solution.py:479
  285.6 73.4 %all-to-all-start.5 = ((bf16[4,1536,256]{2,1,0:T(8,128)(2,1)}), bf16[4,1536,256]{2,1,0:T(8,128)(2,1)S(1)}, u32[]{:S(2)}, u32[]{:S(2)}) async-start(bf16[4,1536,256]{2,1,0:T(8,128)(2,1)} %shard_map.149), calls=%async_computation.6 | async-start | bytes 6291456 | tf_op jit(solution)/shard_map/all_to_all | solution.py:479
  303.4 26.4 %collective-permute-start.39 = (bf16[4,2,256,256]{3,2,1,0:T(8,128)(2,1)}, bf16[4,2,256,256]{3,2,1,0:T(8,128)(2,1)}, u32[]{:S(2)}, u32[]{:S(2)}) collective-permute-start(bf16[4,2,256,256]{3,2,1,0:T(8,128)(2,1)} %get-tuple-element.127), channel_id=1, source_target_pairs={{0,2},{1,3},{2,0},{3,1},{4,6},{5,7},{6,4},{7,5},{8,10},{9,11},{10,... | collective-permute-start | bytes 3145736 | tf_op jit(solution)/shard_map/ppermute | solution.py:444
  304.1 46.9 %collective-permute-start.40 = (bf16[4,2,256,256]{3,2,1,0:T(8,128)(2,1)}, bf16[4,2,256,256]{3,2,1,0:T(8,128)(2,1)}, u32[]{:S(2)}, u32[]{:S(2)}) collective-permute-start(bf16[4,2,256,256]{3,2,1,0:T(8,128)(2,1)} %get-tuple-element.126), channel_id=1, source_target_pairs={{0,4},{1,5},{2,6},{3,7},{4,0},{5,1},{6,2},{7,3},{8,12},{9,13},{10,... | collective-permute-start | bytes 3145736 | tf_op jit(solution)/shard_map/ppermute | solution.py:444
  305.5 45.5 %collective-permute-start.41 = (bf16[4,2,256,256]{3,2,1,0:T(8,128)(2,1)}, bf16[4,2,256,256]{3,2,1,0:T(8,128)(2,1)}, u32[]{:S(2)}, u32[]{:S(2)}) collective-permute-start(bf16[4,2,256,256]{3,2,1,0:T(8,128)(2,1)} %get-tuple-element.125), channel_id=1, source_target_pairs={{0,6},{1,7},{2,4},{3,5},{4,2},{5,3},{6,0},{7,1},{8,14},{9,15},{10,... | collective-permute-start | bytes 3145736 | tf_op jit(solution)/shard_map/ppermute | solution.py:444
  359.0 29.6 %all-to-all-start.6 = ((bf16[4,256,512]{2,1,0:T(8,128)(2,1)}), bf16[4,256,512]{2,1,0:T(8,128)(2,1)}, u32[]{:S(2)}, u32[]{:S(2)}) async-start(bf16[4,256,512]{2,1,0:T(8,128)(2,1)} %pad_maximum_fusion.4), calls=%async_computation.7 | async-start | bytes 2097152 | tf_op jit(solution)/shard_map/all_to_all | solution.py:479
  (60 other events, 369.6 us)
Sparse Core Ops, SparseCore 0:
  21.9 48.6 all-gather.4
  72.4 64.8 all-gather.6
  226.6 54.2 reduce-scatter.1

commit v4 on v3

--- a/solution.py
+++ b/solution.py
@@ -487,8 +487,16 @@
         return own, swap(lax.dynamic_slice_in_dim(w, (1 - c) * half, half, axis))
 
     def along_ring(line):
-        pieces = [line] + [over_ring(line, m) for m in range(1, 4)]
-        return placed([p[None] for p in pieces], (4,) + line.shape, [(r ^ m,) + (0,) * line.ndim for m in range(4)])
+        pieces, spots = [], []
+        for side, (first, second) in ((0, (1, 2)), (1, (2, 1))):
+            part = line[:, side]
+            one = over_ring(part, first)
+            two = over_ring(part, second)
+            three = over_ring(one, second)
+            for m, p in ((0, part), (first, one), (second, two), (3, three)):
+                pieces.append(p[None, :, None])
+                spots.append((r ^ m, 0, side, 0, 0))
+        return placed(pieces, (4,) + line.shape, spots)
 
     def gathered_late(both):
         return lax.all_gather(lax.all_gather(both, "wide"), "ring")
@@ -510,8 +518,8 @@
     shards = [weights[0]] + [over_wide(weights[0], m) for m in range(1, wide)]
     x = by_half(frames, 0, LENGTH)
     cut = LENGTH // 2
-    x, shards[2], keep = lax.optimization_barrier((x, shards[2], keep))
-    shards[3], second = lax.optimization_barrier((shards[3], second))
+    x, shards[3], keep = lax.optimization_barrier((x, shards[3], keep))
+    x, second = lax.optimization_barrier((x, second))
     shards, grad_out = lax.optimization_barrier((shards, grad_out))
     mats = [None, gathered_late(second)]
     xs = exchange(x)

time: 403 us -> 399 us (0.990)
  waiting for transfers between devices: 144 us -> 137 us
    ppermute x49 -> x52, waiting for transfers between devices: 109 us -> 98.1 us  [send(): return lax.ppermute(x, AXES, pairs)]
    ppermute x49 -> x52, starting transfers between devices: 43.3 us -> 44.4 us  [send(): return lax.ppermute(x, AXES, pairs)]
    dynamic_update_slice x7 -> x11, local copies, waits for them, and re-layouts: 7.85 us -> 8.73 us  [placed(): buf = lax.dynamic_update_slice(buf, piece, spot)]
  transfers between devices with their start and end apart: 59 -> 62, of which waited for: 34 -> 41; matrix products, arithmetic and copies ran while one was open for 11% -> 11% of each run, Pallas kernels for 21% -> 21%
where the time goes in v4:
time: 399 us; the launch traced here: 393 us
  waiting for transfers between devices  137 us (34%)
  Pallas kernels  104 us (26%)
  starting transfers between devices  85.7 us (21%)
  local copies, waits for them, and re-layouts  31.1 us (8%)
  other arithmetic  21.5 us (5%)
  between operations  14.3 us (4%)
    ppermute x52, waiting for transfers between devices, send(): return lax.ppermute(x, AXES, pairs)  98.1 us
    ppermute x52, starting transfers between devices, send(): return lax.ppermute(x, AXES, pairs)  44.4 us
    all_to_all x7, starting transfers between devices, exchange(): return lax.all_to_all(x, 'wide', 0, 0, tiled=True)  41.2 us
    all_to_all x7, waiting for transfers between devices, exchange(): return lax.all_to_all(x, 'wide', 0, 0, tiled=True)  18.7 us
    pallas_call x2, Pallas kernels, product(): pl.pallas_call(functools.partial(product_kernel, by_row), grid=(rows // s...  18.7 us
    pallas_call x2, Pallas kernels, backward(): pl.pallas_call(functools.partial(backward_kernel, count, terms), grid=(ro...  17.3 us
    pallas_call x2, Pallas kernels, outer(): pl.pallas_call(functools.partial(outer_kernel, by_row), grid=(blocks,), i...  16.9 us
    all_gather x2, waiting for transfers between devices, gathered_late(): return lax.all_gather(lax.all_gather(both, 'wide'), 'ring')  15.6 us
  transfers between devices with their start and end apart: 62, of which 41 were waited for; matrix products, arithmetic and copies ran while one was open for 11% of the time, Pallas kernels for 21%

profile of v4, /device:TPU:28, one launch (start us, length us, event | category | flops | bytes accessed | tf_op | source)
XLA Modules:
  0.0 393.2 jit_solution(16294606499351314876)
XLA Ops:
  22.9 7.8 %all-to-all-start = ((bf16[4,1024,256]{2,1,0:T(8,128)(2,1)}), bf16[4,1024,256]{2,1,0:T(8,128)(2,1)}, u32[]{:S(2)}, u32[]{:S(2)}) async-start(bf16[4,1024,256]{2,1,0:T(8,128)(2,1)} %pad_maximum_fusion), calls=%async_computation | async-start | bytes 4194304 | tf_op jit(solution)/shard_map/all_to_all | solution.py:479
  30.8 7.1 %collective-permute-done.5 = bf16[256,512]{1,0:T(8,128)(2,1)} collective-permute-done((bf16[256,512]{1,0:T(8,128)(2,1)S(1)}, bf16[256,512]{1,0:T(8,128)(2,1)}, u32[]{:S(2)}, u32[]{:S(2)}) %collective-permute-start.5) | collective-permute-done | bytes 262176 | tf_op jit(solution)/shard_map/ppermute | solution.py:444
  52.5 5.7 %collective-permute-done.7 = bf16[4,256,256]{2,1,0:T(8,128)(2,1)S(1)} collective-permute-done((bf16[4,256,256]{2,1,0:T(8,128)(2,1)S(1)}, bf16[4,256,256]{2,1,0:T(8,128)(2,1)S(1)}, u32[]{:S(2)}, u32[]{:S(2)}) %collective-permute-start.7) | collective-permute-done | bytes 524320 | tf_op jit(solution)/shard_map/ppermute | solution.py:444
  59.8 11.3 %collective-permute-done.10 = bf16[4,256,256]{2,1,0:T(8,128)(2,1)} collective-permute-done((bf16[4,256,256]{2,1,0:T(8,128)(2,1)}, bf16[4,256,256]{2,1,0:T(8,128)(2,1)}, u32[]{:S(2)}, u32[]{:S(2)}) %collective-permute-start.10) | collective-permute-done | bytes 524320 | tf_op jit(solution)/shard_map/ppermute | solution.py:444
  73.3 8.2 %collective-permute-done.9 = bf16[4,256,256]{2,1,0:T(8,128)(2,1)S(1)} collective-permute-done((bf16[4,256,256]{2,1,0:T(8,128)(2,1)S(1)}, bf16[4,256,256]{2,1,0:T(8,128)(2,1)S(1)}, u32[]{:S(2)}, u32[]{:S(2)}) %collective-permute-start.9) | collective-permute-done | bytes 524320 | tf_op jit(solution)/shard_map/ppermute | solution.py:444
  83.2 10.1 %all-gather.5.cloned.1.call-done = bf16[8,256,256]{2,1,0:T(8,128)(2,1)} async-done(((bf16[2,256,256]{2,1,0:T(8,128)(2,1)}), bf16[8,256,256]{2,1,0:T(8,128)(2,1)}) %all-gather.5.cloned.1.call-update) | async-done | bytes 1048592 | tf_op jit(solution)/shard_map/all_gather | solution.py:502
  104.4 9.5 %shard_map.135 = (f32[8192,128]{1,0:T(8,128)}, f32[2,8,128]{2,1,0:T(8,128)}) custom-call(bf16[4,1024,256]{2,1,0:T(8,128)(2,1)} %all-to-all-done.xs, bf16[4,1024,256]{2,1,0:T(8,128)(2,1)} %collective-permute-done.14.xo, bf16[4,4,2,256,256]{4,3,2,1,0:T(8,128)(2,1)} %bitcast_dynamic-update-slice_fusion.7.w), custom_call_target="tpu_custom_call" | custom-call | flops 4294967296 | bytes 12582912 | tf_op jit(solution)/shard_map/pallas_call | solution.py:66
  131.4 6.2 %shard_map.136 = (f32[8192,128]{1,0:T(8,128)}, bf16[4,1024,256]{2,1,0:T(8,128)(2,1)}) custom-call(f32[2,8,128]{2,1,0:T(8,128)} %fusion.12.sums, f32[3,8,128]{2,1,0:T(8,128)} %get-tuple-element.150.params, f32[1024]{0:T(1024)} %fusion.22.keep, f32[8192,128]{1,0:T(8,128)} %get-tuple-element.72.pre), custom_call_target="tpu_custom_call" | custom-call | flops 12582912 | bytes 10485760 | tf_op jit(solution)/shard_map/pallas_call | solution.py:143
  137.6 5.9 %all-to-all-start.3 = ((bf16[4,512,256]{2,1,0:T(8,128)(2,1)}), bf16[4,512,256]{2,1,0:T(8,128)(2,1)S(1)}, u32[]{:S(2)}, u32[]{:S(2)}) async-start(bf16[4,512,256]{2,1,0:T(8,128)(2,1)} %pad_maximum_fusion.3), calls=%async_computation.3 | async-start | bytes 2097152 | tf_op jit(solution)/shard_map/all_to_all | solution.py:479
  143.5 5.5 %all-gather.7.cloned.1.call-done = bf16[16,2,256,256]{3,2,1,0:T(8,128)(2,1)} async-done(((bf16[4,2,256,256]{3,2,1,0:T(8,128)(2,1)}), bf16[16,2,256,256]{3,2,1,0:T(8,128)(2,1)}) %all-gather.7.cloned.1.call-update) | async-done | bytes 4194320 | tf_op jit(solution)/shard_map/all_gather | solution.py:502
  149.0 9.1 %shard_map.137 = (f32[8192,128]{1,0:T(8,128)}, f32[2,8,128]{2,1,0:T(8,128)}) custom-call(bf16[4,1024,256]{2,1,0:T(8,128)(2,1)} %get-tuple-element.73.xs, bf16[4,1024,256]{2,1,0:T(8,128)(2,1)} %collective-permute-done.22.xo, bf16[4,4,2,256,256]{4,3,2,1,0:T(8,128)(2,1)} %bitcast.103), custom_call_target="tpu_custom_call" | custom-call | flops 4294967296 | bytes 12582912 | tf_op jit(solution)/shard_map/pallas_call | solution.py:66
  171.9 6.5 %shard_map.138 = (f32[8192,128]{1,0:T(8,128)}, bf16[4,512,256]{2,1,0:T(8,128)(2,1)}, bf16[4,512,256]{2,1,0:T(8,128)(2,1)}) custom-call(f32[2,8,128]{2,1,0:T(8,128)} %add_add_fusion.4.sums, f32[3,8,128]{2,1,0:T(8,128)} %get-tuple-element.149.params, f32[1024]{0:T(1024)} %fusion.22.keep, f32[8192,128]{1,0:T(8,128)} %get-tuple-element.76.pre), custom_call_target="tpu_custom_call" | custom-call | flops 12582912 | bytes 10485760 | tf_op jit(solution)/shard_map/pallas_call | solution.py:143
  183.7 8.3 %shard_map.139 = (f32[8192,128]{1,0:T(8,128)}, f32[3,8,128]{2,1,0:T(8,128)}) custom-call(f32[2,8,128]{2,1,0:T(8,128)} %add_add_fusion.4.sums, f32[3,8,128]{2,1,0:T(8,128)} %get-tuple-element.149.params, f32[1024]{0:T(1024)} %fusion.22.keep, f32[8192,128]{1,0:T(8,128)} %get-tuple-element.76.pre, f32[8192,128]{1,0:T(8,128)} %get-tuple-element.79.states.before, ...), custom_call_target="tpu_custom_call" | custom-call | flops 25165824 | bytes 16777216 | tf_op jit(solution)/shard_map/pallas_call | solution.py:245
  206.8 7.5 %shard_map.140 = (bf16[1024,1024]{1,0:T(8,128)(2,1)}, bf16[4,1024,256]{2,1,0:T(8,128)(2,1)}) custom-call(f32[2,8,128]{2,1,0:T(8,128)} %add_add_fusion.4.sums, f32[3,8,128]{2,1,0:T(8,128)} %get-tuple-element.149.params, f32[3,8,128]{2,1,0:T(8,128)} %add_add_fusion.2.totals, f32[8192,128]{1,0:T(8,128)} %get-tuple-element.87.carried, ...), custom_call_target="tpu_custom_call" | custom-call | flops 2147483648 | bytes 16777216 | tf_op jit(solution)/shard_map/pallas_call | solution.py:305
  214.3 8.5 %shard_map.141 = bf16[4,4,2,256,256]{4,3,2,1,0:T(8,128)(2,1)} custom-call(bf16[4,1024,256]{2,1,0:T(8,128)(2,1)} %get-tuple-element.73.xs, bf16[4,1024,256]{2,1,0:T(8,128)(2,1)} %collective-permute-done.22.xo, bf16[1024,1024]{1,0:T(8,128)(2,1)} %get-tuple-element.89.dpre), custom_call_target="tpu_custom_call" | custom-call | flops 4294967296 | bytes 10485760 | tf_op jit(solution)/shard_map/pallas_call | solution.py:383
  228.3 5.5 %shard_map.142.rest_0_ = bf16[4,1024,256]{2,1,0:T(8,128)(2,1)} custom-call(bf16[1024,1024]{1,0:T(8,128)(2,1)} %get-tuple-element.89.dpre, bf16[4,4,2,256,256]{4,3,2,1,0:T(8,128)(2,1)} %bitcast.105), custom_call_target="tpu_custom_call" | custom-call | flops 2147483648 | bytes 6291456 | tf_op jit(solution)/shard_map/pallas_call | solution.py:332
  235.1 9.0 %shard_map.143 = (f32[8192,128]{1,0:T(8,128)}, f32[3,8,128]{2,1,0:T(8,128)}) custom-call(f32[2,8,128]{2,1,0:T(8,128)} %fusion.12.sums, f32[3,8,128]{2,1,0:T(8,128)} %get-tuple-element.150.params, f32[1024]{0:T(1024)} %fusion.22.keep, f32[8192,128]{1,0:T(8,128)} %get-tuple-element.72.pre, f32[8192,128]{1,0:T(8,128)} %get-tuple-element.85.states.before, ...), custom_call_target="tpu_custom_call" | custom-call | flops 25165824 | bytes 16777216 | tf_op jit(solution)/shard_map/pallas_call | solution.py:245
  259.0 7.7 %shard_map.144 = (bf16[1024,1024]{1,0:T(8,128)(2,1)}, bf16[4,1024,256]{2,1,0:T(8,128)(2,1)}) custom-call(f32[2,8,128]{2,1,0:T(8,128)} %fusion.12.sums, f32[3,8,128]{2,1,0:T(8,128)} %get-tuple-element.150.params, f32[3,8,128]{2,1,0:T(8,128)} %add_add_fusion.totals, f32[8192,128]{1,0:T(8,128)} %get-tuple-element.93.carried, ...), custom_call_target="tpu_custom_call" | custom-call | flops 2147483648 | bytes 16777216 | tf_op jit(solution)/shard_map/pallas_call | solution.py:305
  266.8 5.6 %shard_map.148.same = bf16[4,1024,256]{2,1,0:T(8,128)(2,1)} custom-call(bf16[1024,1024]{1,0:T(8,128)(2,1)} %get-tuple-element.94.dpre, bf16[4,4,2,256,256]{4,3,2,1,0:T(8,128)(2,1)} %bitcast_dynamic-update-slice_fusion.7.w), custom_call_target="tpu_custom_call" | custom-call | flops 2147483648 | bytes 6291456 | tf_op jit(solution)/shard_map/pallas_call | solution.py:332
  286.4 8.4 %shard_map.145 = bf16[4,4,2,256,256]{4,3,2,1,0:T(8,128)(2,1)} custom-call(bf16[4,1024,256]{2,1,0:T(8,128)(2,1)} %all-to-all-done.xs, bf16[4,1024,256]{2,1,0:T(8,128)(2,1)} %collective-permute-done.14.xo, bf16[1024,1024]{1,0:T(8,128)(2,1)} %get-tuple-element.94.dpre), custom_call_target="tpu_custom_call" | custom-call | flops 4294967296 | bytes 10485760 | tf_op jit(solution)/shard_map/pallas_call | solution.py:383
  311.3 14.2 %collective-permute-done.42 = bf16[4,2,256,256]{3,2,1,0:T(8,128)(2,1)} collective-permute-done((bf16[4,2,256,256]{3,2,1,0:T(8,128)(2,1)}, bf16[4,2,256,256]{3,2,1,0:T(8,128)(2,1)}, u32[]{:S(2)}, u32[]{:S(2)}) %collective-permute-start.42) | collective-permute-done | bytes 1048608 | tf_op jit(solution)/shard_map/ppermute | solution.py:444
  325.5 21.1 %collective-permute-done.43 = bf16[4,2,256,256]{3,2,1,0:T(8,128)(2,1)} collective-permute-done((bf16[4,2,256,256]{3,2,1,0:T(8,128)(2,1)}, bf16[4,2,256,256]{3,2,1,0:T(8,128)(2,1)}, u32[]{:S(2)}, u32[]{:S(2)}) %collective-permute-start.43) | collective-permute-done | bytes 1048608 | tf_op jit(solution)/shard_map/ppermute | solution.py:444
  354.7 6.6 %all-to-all-start.6 = ((bf16[4,256,512]{2,1,0:T(8,128)(2,1)}), bf16[4,256,512]{2,1,0:T(8,128)(2,1)}, u32[]{:S(2)}, u32[]{:S(2)}) async-start(bf16[4,256,512]{2,1,0:T(8,128)(2,1)} %pad_maximum_fusion.4), calls=%async_computation.7 | async-start | bytes 2097152 | tf_op jit(solution)/shard_map/all_to_all | solution.py:479
  369.4 14.8 %all-to-all-done.6 = bf16[4,256,512]{2,1,0:T(8,128)(2,1)} async-done(((bf16[4,256,512]{2,1,0:T(8,128)(2,1)}), bf16[4,256,512]{2,1,0:T(8,128)(2,1)}, u32[]{:S(2)}, u32[]{:S(2)}) %all-to-all-start.6) | async-done | bytes 1048608 | tf_op jit(solution)/shard_map/all_to_all | solution.py:479
  (245 shorter events, 168.7 us)
Async XLA Ops:
  9.6 8.9 %collective-permute-start = (bf16[2,1024,256]{2,1,0:T(8,128)(2,1)}, bf16[2,1024,256]{2,1,0:T(8,128)(2,1)S(1)}, u32[]{:S(2)}, u32[]{:S(2)}) collective-permute-start(bf16[2,1024,256]{2,1,0:T(8,128)(2,1)} %constant_dynamic-slice_fusion.7), channel_id=1, source_target_pairs={{0,1},{1,0},{2,3},{3,2},{4,5},{5,4},{6,7},{7,6},{8,9},{9,8},{10,11... | collective-permute-start | bytes 3145736 | tf_op jit(solution)/shard_map/ppermute | solution.py:444
  11.9 11.1 %collective-permute-start.1 = (bf16[256,512]{1,0:T(8,128)(2,1)S(1)}, bf16[256,512]{1,0:T(8,128)(2,1)}, u32[]{:S(2)}, u32[]{:S(2)}) collective-permute-start(bf16[256,512]{1,0:T(8,128)(2,1)S(1)} %get-tuple-element.61), channel_id=1, source_target_pairs={{0,24},{1,25},{2,26},{3,27},{4,28},{5,29},{6,30},{7,31},{8,16},{9,... | collective-permute-start | bytes 786440 | tf_op jit(solution)/shard_map/ppermute | solution.py:444
  12.1 18.7 %collective-permute-start.4 = (bf16[256,512]{1,0:T(8,128)(2,1)S(1)}, bf16[256,512]{1,0:T(8,128)(2,1)}, u32[]{:S(2)}, u32[]{:S(2)}) collective-permute-start(bf16[256,512]{1,0:T(8,128)(2,1)S(1)} %get-tuple-element.61), channel_id=1, source_target_pairs={{0,8},{1,9},{2,10},{3,11},{4,12},{5,13},{6,14},{7,15},{8,0},{9,1},... | collective-permute-start | bytes 786440 | tf_op jit(solution)/shard_map/ppermute | solution.py:444
  13.0 24.9 %collective-permute-start.5 = (bf16[256,512]{1,0:T(8,128)(2,1)S(1)}, bf16[256,512]{1,0:T(8,128)(2,1)}, u32[]{:S(2)}, u32[]{:S(2)}) collective-permute-start(bf16[256,512]{1,0:T(8,128)(2,1)S(1)} %get-tuple-element.61), channel_id=1, source_target_pairs={{0,16},{1,17},{2,18},{3,19},{4,20},{5,21},{6,22},{7,23},{8,24},{9,... | collective-permute-start | bytes 786440 | tf_op jit(solution)/shard_map/ppermute | solution.py:444
  22.9 76.4 %all-to-all-start = ((bf16[4,1024,256]{2,1,0:T(8,128)(2,1)}), bf16[4,1024,256]{2,1,0:T(8,128)(2,1)}, u32[]{:S(2)}, u32[]{:S(2)}) async-start(bf16[4,1024,256]{2,1,0:T(8,128)(2,1)} %pad_maximum_fusion), calls=%async_computation | async-start | bytes 4194304 | tf_op jit(solution)/shard_map/all_to_all | solution.py:479
  30.8 62.5 %all-gather.5.cloned.1.call-start = ((), (), s32[]{:S(2)}) async-start(), calls=%async_computation.9 | async-start | bytes 1310720 | tf_op jit(solution)/shard_map/all_gather | solution.py:502
  42.4 106.6 %all-gather.7.cloned.1.call-start = ((), (), s32[]{:S(2)}) async-start(), calls=%async_computation.10 | async-start | bytes 5242880 | tf_op jit(solution)/shard_map/all_gather | solution.py:502
  43.5 14.7 %collective-permute-start.7 = (bf16[4,256,256]{2,1,0:T(8,128)(2,1)S(1)}, bf16[4,256,256]{2,1,0:T(8,128)(2,1)S(1)}, u32[]{:S(2)}, u32[]{:S(2)}) collective-permute-start(bf16[4,256,256]{2,1,0:T(8,128)(2,1)S(1)} %get-tuple-element.140), channel_id=1, source_target_pairs={{0,2},{1,3},{2,0},{3,1},{4,6},{5,7},{6,4},{7,5},{8,10},{9,11},{10,... | collective-permute-start | bytes 1572872 | tf_op jit(solution)/shard_map/ppermute | solution.py:444
  45.0 27.5 %collective-permute-start.8 = (bf16[4,256,256]{2,1,0:T(8,128)(2,1)S(1)}, bf16[4,256,256]{2,1,0:T(8,128)(2,1)S(1)}, u32[]{:S(2)}, u32[]{:S(2)}) collective-permute-start(bf16[4,256,256]{2,1,0:T(8,128)(2,1)S(1)} %get-tuple-element.140), channel_id=1, source_target_pairs={{0,4},{1,5},{2,6},{3,7},{4,0},{5,1},{6,2},{7,3},{8,12},{9,13},{10,... | collective-permute-start | bytes 1572872 | tf_op jit(solution)/shard_map/ppermute | solution.py:444
  45.5 25.6 %collective-permute-start.10 = (bf16[4,256,256]{2,1,0:T(8,128)(2,1)}, bf16[4,256,256]{2,1,0:T(8,128)(2,1)}, u32[]{:S(2)}, u32[]{:S(2)}) collective-permute-start(bf16[4,256,256]{2,1,0:T(8,128)(2,1)} %get-tuple-element.139), channel_id=1, source_target_pairs={{0,4},{1,5},{2,6},{3,7},{4,0},{5,1},{6,2},{7,3},{8,12},{9,13},{10,... | collective-permute-start | bytes 1572872 | tf_op jit(solution)/shard_map/ppermute | solution.py:444
  47.0 48.1 %collective-permute-start.11 = (bf16[4,256,256]{2,1,0:T(8,128)(2,1)}, bf16[4,256,256]{2,1,0:T(8,128)(2,1)}, u32[]{:S(2)}, u32[]{:S(2)}) collective-permute-start(bf16[4,256,256]{2,1,0:T(8,128)(2,1)} %get-tuple-element.139), channel_id=1, source_target_pairs={{0,2},{1,3},{2,0},{3,1},{4,6},{5,7},{6,4},{7,5},{8,10},{9,11},{10,... | collective-permute-start | bytes 1572872 | tf_op jit(solution)/shard_map/ppermute | solution.py:444
  58.2 23.3 %collective-permute-start.9 = (bf16[4,256,256]{2,1,0:T(8,128)(2,1)S(1)}, bf16[4,256,256]{2,1,0:T(8,128)(2,1)S(1)}, u32[]{:S(2)}, u32[]{:S(2)}) collective-permute-start(bf16[4,256,256]{2,1,0:T(8,128)(2,1)S(1)} %collective-permute-done.7), channel_id=1, source_target_pairs={{0,4},{1,5},{2,6},{3,7},{4,0},{5,1},{6,2},{7,3},{8,12},{9,13},{10,... | collective-permute-start | bytes 1572872 | tf_op jit(solution)/shard_map/ppermute | solution.py:444
  71.1 26.0 %collective-permute-start.12 = (bf16[4,256,256]{2,1,0:T(8,128)(2,1)}, bf16[4,256,256]{2,1,0:T(8,128)(2,1)S(1)}, u32[]{:S(2)}, u32[]{:S(2)}) collective-permute-start(bf16[4,256,256]{2,1,0:T(8,128)(2,1)} %collective-permute-done.10), channel_id=1, source_target_pairs={{0,2},{1,3},{2,0},{3,1},{4,6},{5,7},{6,4},{7,5},{8,10},{9,11},{10,... | collective-permute-start | bytes 1572872 | tf_op jit(solution)/shard_map/ppermute | solution.py:444
  99.3 31.2 %all-to-all-start.1 = ((bf16[4,512,256]{2,1,0:T(8,128)(2,1)}), bf16[4,512,256]{2,1,0:T(8,128)(2,1)S(1)}, u32[]{:S(2)}, u32[]{:S(2)}) async-start(bf16[4,512,256]{2,1,0:T(8,128)(2,1)} %pad_maximum_fusion.2), calls=%async_computation.1 | async-start | bytes 2097152 | tf_op jit(solution)/shard_map/all_to_all | solution.py:479
  137.6 40.8 %all-to-all-start.3 = ((bf16[4,512,256]{2,1,0:T(8,128)(2,1)}), bf16[4,512,256]{2,1,0:T(8,128)(2,1)S(1)}, u32[]{:S(2)}, u32[]{:S(2)}) async-start(bf16[4,512,256]{2,1,0:T(8,128)(2,1)} %pad_maximum_fusion.3), calls=%async_computation.3 | async-start | bytes 2097152 | tf_op jit(solution)/shard_map/all_to_all | solution.py:479
  178.4 28.4 %all-to-all-start.2 = ((bf16[4,512,256]{2,1,0:T(8,128)(2,1)}), bf16[4,512,256]{2,1,0:T(8,128)(2,1)S(1)}, u32[]{:S(2)}, u32[]{:S(2)}) async-start(bf16[4,512,256]{2,1,0:T(8,128)(2,1)} %get-tuple-element.77), calls=%async_computation.2 | async-start | bytes 2097152 | tf_op jit(solution)/shard_map/all_to_all | solution.py:479
  183.7 92.9 %reduce-scatter.2.cloned.1.call-start = ((), (), s32[]{:S(2)}) async-start(), calls=%async_computation.8 | async-start | bytes 5242880 | tf_op jit(solution)/shard_map/reduce_scatter | solution.py:509
  222.8 11.0 %collective-permute-start.35 = (bf16[4,1024,256]{2,1,0:T(8,128)(2,1)}, bf16[4,1024,256]{2,1,0:T(8,128)(2,1)S(1)}, u32[]{:S(2)}, u32[]{:S(2)}) collective-permute-start(bf16[4,1024,256]{2,1,0:T(8,128)(2,1)} %get-tuple-element.90), channel_id=1, source_target_pairs={{0,1},{1,0},{2,3},{3,2},{4,5},{5,4},{6,7},{7,6},{8,9},{9,8},{10,11... | collective-permute-start | bytes 6291464 | tf_op jit(solution)/shard_map/ppermute | solution.py:444
  222.9 36.2 %all-to-all-start.4 = ((bf16[4,512,256]{2,1,0:T(8,128)(2,1)}), bf16[4,512,256]{2,1,0:T(8,128)(2,1)S(1)}, u32[]{:S(2)}, u32[]{:S(2)}) async-start(bf16[4,512,256]{2,1,0:T(8,128)(2,1)} %get-tuple-element.84), calls=%async_computation.4 | async-start | bytes 2097152 | tf_op jit(solution)/shard_map/all_to_all | solution.py:479
  281.3 73.4 %all-to-all-start.5 = ((bf16[4,1536,256]{2,1,0:T(8,128)(2,1)}), bf16[4,1536,256]{2,1,0:T(8,128)(2,1)S(1)}, u32[]{:S(2)}, u32[]{:S(2)}) async-start(bf16[4,1536,256]{2,1,0:T(8,128)(2,1)} %shard_map.149), calls=%async_computation.6 | async-start | bytes 6291456 | tf_op jit(solution)/shard_map/all_to_all | solution.py:479
  299.1 26.4 %collective-permute-start.42 = (bf16[4,2,256,256]{3,2,1,0:T(8,128)(2,1)}, bf16[4,2,256,256]{3,2,1,0:T(8,128)(2,1)}, u32[]{:S(2)}, u32[]{:S(2)}) collective-permute-start(bf16[4,2,256,256]{3,2,1,0:T(8,128)(2,1)} %get-tuple-element.127), channel_id=1, source_target_pairs={{0,2},{1,3},{2,0},{3,1},{4,6},{5,7},{6,4},{7,5},{8,10},{9,11},{10,... | collective-permute-start | bytes 3145736 | tf_op jit(solution)/shard_map/ppermute | solution.py:444
  299.7 46.9 %collective-permute-start.43 = (bf16[4,2,256,256]{3,2,1,0:T(8,128)(2,1)}, bf16[4,2,256,256]{3,2,1,0:T(8,128)(2,1)}, u32[]{:S(2)}, u32[]{:S(2)}) collective-permute-start(bf16[4,2,256,256]{3,2,1,0:T(8,128)(2,1)} %get-tuple-element.126), channel_id=1, source_target_pairs={{0,4},{1,5},{2,6},{3,7},{4,0},{5,1},{6,2},{7,3},{8,12},{9,13},{10,... | collective-permute-start | bytes 3145736 | tf_op jit(solution)/shard_map/ppermute | solution.py:444
  301.1 45.5 %collective-permute-start.44 = (bf16[4,2,256,256]{3,2,1,0:T(8,128)(2,1)}, bf16[4,2,256,256]{3,2,1,0:T(8,128)(2,1)}, u32[]{:S(2)}, u32[]{:S(2)}) collective-permute-start(bf16[4,2,256,256]{3,2,1,0:T(8,128)(2,1)} %get-tuple-element.125), channel_id=1, source_target_pairs={{0,6},{1,7},{2,4},{3,5},{4,2},{5,3},{6,0},{7,1},{8,14},{9,15},{10,... | collective-permute-start | bytes 3145736 | tf_op jit(solution)/shard_map/ppermute | solution.py:444
  354.7 29.6 %all-to-all-start.6 = ((bf16[4,256,512]{2,1,0:T(8,128)(2,1)}), bf16[4,256,512]{2,1,0:T(8,128)(2,1)}, u32[]{:S(2)}, u32[]{:S(2)}) async-start(bf16[4,256,512]{2,1,0:T(8,128)(2,1)} %pad_maximum_fusion.4), calls=%async_computation.7 | async-start | bytes 2097152 | tf_op jit(solution)/shard_map/all_to_all | solution.py:479
  (60 other events, 343.0 us)
Sparse Core Ops, SparseCore 0:
  42.5 50.7 all-gather.4
  95.1 53.7 all-gather.6
  222.9 53.6 reduce-scatter.1
